TPU v7x, 128 devices: a whole 4x4x4 slice. The times are simulated.
128 devices in a mesh: band: 16 (over x, y), chan: 8 (over z, core).
Axes of the slice: x: 4, y: 4, z: 4, core: 2. Of those that a mesh axis runs over, the one named last changes fastest.
Arguments:
- analysed_fields: float32 [227, 32, 1024], P(None, 'band'), may hold values from -6 to 6
- prediction_adjoint_seed: float32 [227, 32, 1024], P(None, 'band'), may hold values from -6 to 6
- encoder_kernel_matrix: bfloat16 [512, 227, 3, 3], P('chan'), may hold values from -0.125 to 0.125
- hidden_offset_term: float32 [512], P('chan'), may hold values from -1 to 1
- decoder_kernel_matrix: bfloat16 [227, 512, 3, 3], P(None, 'chan'), may hold values from -0.09375 to 0.09375
- measurement_wanted_positions: int32 [16, 8, 16, 256], P('band', 'chan'), may hold values from 0 to 32767
- measurement_active_total: int32 [16, 8, 16], P('band', 'chan'), may hold values from 1 to 256, as said below
- measurement_linear_operator: bfloat16 [16, 8, 227, 16, 256], P('band', 'chan'), may hold values from -0.375 to 0.375
Outputs:
- analysis_sensitivity: float32 [227, 32, 1024], P(None, 'band', 'chan')
- obs_impact: float32 [16, 8, 16, 256], P('band', 'chan')
Inputs may be any that keep to these rules, and one draw needn't show every extreme that they name: Live slots of each row are the first measurement_active_total of them; 256 is reached in every draw. `measurement_wanted_positions`: position inside target band k on a grid refined 4 times in both directions: fine_row * 1024 * 4 + fine_lon. Slots past the count hold positions as well.
All inputs are finite; a program needn't handle non-finite values.
Results may differ from a plain program's by a relative error of at most 0.015.
Values may be sent and summed in bfloat16 or wider, within the bound.
A program may use at most 128 MiB of HBM per device.

v0:
```python
import jax
import jax.numpy as jnp
from jax import lax
from jax.sharding import PartitionSpec as P

SUBCELLS = 4


def with_halo(array, sides, width):
    for axis, dim in sides:
        size, length = (lax.axis_size(axis), array.shape[dim])
        up = [(i, (i + 1) % size) for i in range(size - 1)]
        down = [(j, i) for i, j in up]
        last = lax.slice_in_dim(array, length - width, length, axis=dim)
        first = lax.slice_in_dim(array, 0, width, axis=dim)
        before = lax.ppermute(last, axis, up)
        after = lax.ppermute(first, axis, down)
        array = jnp.concatenate([before, array, after], axis=dim)
    return array


def as_sent(array):
    return jax.tree.map(lambda a: a.astype(jnp.bfloat16) if a.dtype == jnp.float32 else a, array)


def shifted(array, axis, by):
    size = lax.axis_size(axis)
    pairs = [(i, i + by) for i in range(size) if 0 <= i + by < size]
    return lax.ppermute(array, axis, pairs)


def convolve(extended, kernel):
    wrapped = jnp.concatenate([extended[:, :, -1:], extended, extended[:, :, :1]], axis=2)
    result = lax.conv_general_dilated(
        wrapped[None],
        kernel,
        (1, 1),
        "VALID",
        dimension_numbers=("NCHW", "OIHW", "NCHW"),
        preferred_element_type=jnp.float32,
    )
    return result[0]


def flipped(kernel):
    return jnp.swapaxes(kernel, 0, 1)[:, :, ::-1, ::-1]


def silu_slope(preact):
    logistic = jax.nn.sigmoid(preact)
    return logistic * (1.0 + preact * (1.0 - logistic))


def latent_halo(values):
    return with_halo(values, (("band", 1),), 1)


def append_next(values):
    below = shifted(as_sent(values[:, :1, :]), "band", -1)
    return jnp.concatenate([values, below], axis=1)


def interpolate(flat, positions, first_row, span):
    fine_row = positions // (span * SUBCELLS)
    fine_lon = positions % (span * SUBCELLS)
    north = first_row + fine_row // SUBCELLS
    west = fine_lon // SUBCELLS
    east = (west + 1) % span
    row_frac = (fine_row % SUBCELLS).astype(jnp.float32) / SUBCELLS
    lon_frac = (fine_lon % SUBCELLS).astype(jnp.float32) / SUBCELLS
    corner_nw = jnp.take(flat, north * span + west, axis=1)
    corner_ne = jnp.take(flat, north * span + east, axis=1)
    corner_sw = jnp.take(flat, (north + 1) * span + west, axis=1)
    corner_se = jnp.take(flat, (north + 1) * span + east, axis=1)
    mixed = (
        (1.0 - row_frac) * (1.0 - lon_frac) * corner_nw
        + (1.0 - row_frac) * lon_frac * corner_ne
        + row_frac * (1.0 - lon_frac) * corner_sw
        + row_frac * lon_frac * corner_se
    )
    return mixed.astype(jnp.bfloat16)


def local(
    analysed_fields,
    prediction_adjoint_seed,
    encoder_kernel_matrix,
    hidden_offset_term,
    decoder_kernel_matrix,
    measurement_wanted_positions,
    measurement_active_total,
    measurement_linear_operator,
):
    span = analysed_fields.shape[2]
    share = span // lax.axis_size("chan")
    offset = lax.axis_index("chan") * share
    positions = measurement_wanted_positions[0, 0]
    counts = measurement_active_total[0, 0]
    jacobian = measurement_linear_operator[0, 0]
    asked = lax.all_to_all(positions, "band", split_axis=0, concat_axis=0, tiled=True)

    def extend_state(values):
        return with_halo(values.astype(jnp.bfloat16), (("band", 1),), 1)

    def combine_sums(values, partial_value):
        return values + lax.psum(partial_value.astype(jnp.bfloat16), "chan").astype(jnp.float32)

    derivative_mapping = prediction_adjoint_seed
    bias = hidden_offset_term[:, None, None]
    first_pre = convolve(extend_state(analysed_fields), encoder_kernel_matrix) + bias
    first_hidden = (first_pre * jax.nn.sigmoid(first_pre)).astype(jnp.bfloat16)
    second_state = combine_sums(
        analysed_fields, convolve(latent_halo(first_hidden), decoder_kernel_matrix)
    )
    second_pre = convolve(extend_state(second_state), encoder_kernel_matrix) + bias
    out_flip = flipped(decoder_kernel_matrix)
    in_flip = flipped(encoder_kernel_matrix)
    for preact in (second_pre, first_pre):
        latent_grad = convolve(extend_state(derivative_mapping), out_flip)
        slope = (latent_grad * silu_slope(preact)).astype(jnp.bfloat16)
        derivative_mapping = combine_sums(derivative_mapping, convolve(latent_halo(slope), in_flip))
    grid = append_next(derivative_mapping)
    sensitivity = lax.dynamic_slice_in_dim(derivative_mapping, offset, share, 2)
    flat = grid.reshape(grid.shape[0], -1)
    columns = interpolate(flat, asked, 0, span)
    returned = lax.all_to_all(columns, "band", split_axis=1, concat_axis=1, tiled=True)
    impact = jnp.einsum("cks,cks->ks", returned, jacobian, preferred_element_type=jnp.float32)
    slots = positions.shape[1]
    live = jnp.arange(slots, dtype=jnp.int32)[None, :] < counts[:, None]
    obs_impact = jnp.where(live, impact, jnp.float32(0.0))
    return (sensitivity, obs_impact[None, None])


def solution(mesh):
    in_specs = (
        P(None, "band", None),
        P(None, "band", None),
        P("chan", None, None, None),
        P("chan"),
        P(None, "chan", None, None),
        P("band", "chan", None, None),
        P("band", "chan", None),
        P("band", "chan", None, None, None),
    )
    out_specs = (P(None, "band", "chan"), P("band", "chan", None, None))
    return jax.shard_map(local, mesh=mesh, in_specs=in_specs, out_specs=out_specs, check_vma=False)
```

profile of v0, /device:TPU:1, one launch (start us, length us, event | category | flops | bytes accessed | tf_op | source)
XLA Modules:
  0.0 597.8 jit_solution(959304020510060335)
XLA Ops:
  16.0 7.7 %collective-permute-done.3 = bf16[227,1,1024]{2,0,1:T(8,128)(2,1)S(1)} collective-permute-done((bf16[227,1,1024]{2,0,1:T(8,128)(2,1)S(1)}, bf16[227,1,1024]{2,0,1:T(8,128)(2,1)S(1)}, u32[]{:S(2)}, u32[]{:S(2)}) %collective-permute-start.3) | collective-permute-done | bytes 464928 | tf_op jit(solution)/shard_map/ppermute | solution.py:17
  31.9 5.8 reshape.290
  37.7 5.3 copy.45
  57.8 16.4 %collective-permute-start = (bf16[227,1,1024]{2,0,1:T(8,128)(2,1)}, bf16[227,1,1024]{2,0,1:T(8,128)(2,1)}, u32[]{:S(2)}, u32[]{:S(2)}) collective-permute-start(bf16[227,1,1024]{2,0,1:T(8,128)(2,1)} %get-tuple-element.28), channel_id=1, source_target_pairs={{0,8},{8,16},{16,24},{24,32},{32,40},{40,48},{48,56},{56,64},{64,7... | collective-permute-start | bytes 1394696 | tf_op jit(solution)/shard_map/ppermute | solution.py:16
  87.8 67.1 %all-reduce.4.cloned.1.call-done = bf16[227,2,1024]{0,2,1:T(8,128)(2,1)} async-done(((bf16[227,2,1024]{0,2,1:T(8,128)(2,1)}), bf16[227,2,1024]{0,2,1:T(8,128)(2,1)}) %all-reduce.4.cloned.1.call-update) | async-done | bytes 929808 | tf_op jit(solution)/shard_map/psum | solution.py:106
  172.6 7.2 %reshape.289 = bf16[227,4,1,8,129]{4,3,0,1,2:T(8,128)(2,1)} reshape(bf16[227,4,1,1032]{3,0,1,2:T(8,128)(2,1)} %pad) | data formatting | bytes 3748224 | tf_op jit(solution)/shard_map/conv_general_dilated | solution.py:34
  179.8 6.4 %copy.40 = bf16[227,4,1,8,129]{0,3,4,1,2:T(8,128)(2,1)} copy(bf16[227,4,1,8,129]{4,3,0,1,2:T(8,128)(2,1)} %reshape.289) | data formatting | bytes 3748224 | tf_op jit(solution)/shard_map/conv_general_dilated | solution.py:34
  198.3 10.5 %concatenate.52 = bf16[227,4,1026]{0,2,1:T(8,128)(2,1)S(1)} concatenate(bf16[227,4,1]{0,2,1:T(2,128)(2,1)S(1)} %get-tuple-element.17, bf16[227,4,1024]{0,2,1:T(8,128)(2,1)} %copy-done.3, bf16[227,4,1]{0,2,1:T(2,128)(2,1)S(1)} %get-tuple-element.16), dimensions={2} | concatenate | bytes 3726432 | tf_op jit(solution)/shard_map/concatenate | solution.py:33
  232.6 10.4 %all-to-all-start = ((s32[16,1,256]{2,1,0:T(1,128)}), s32[16,1,256]{2,1,0:T(1,128)S(1)}, u32[]{:S(2)}, u32[]{:S(2)}) async-start(s32[16,1,256]{2,1,0:T(1,128)} %all_to_all.11), calls=%async_computation | async-start | bytes 32768 | tf_op jit(solution)/shard_map/all_to_all | solution.py:100
  245.7 54.0 %all-reduce.6.cloned.1.call-done = bf16[227,2,1024]{0,2,1:T(8,128)(2,1)} async-done(((bf16[227,2,1024]{0,2,1:T(8,128)(2,1)}), bf16[227,2,1024]{0,2,1:T(8,128)(2,1)}) %all-reduce.6.cloned.1.call-update) | async-done | bytes 929808 | tf_op jit(solution)/shard_map/psum | solution.py:106
  319.0 13.7 %concatenate.56 = bf16[227,4,1026]{0,2,1:T(8,128)(2,1)} concatenate(bf16[227,4,1]{0,2,1:T(2,128)(2,1)S(1)} %get-tuple-element.15, bf16[227,4,1024]{0,2,1:T(8,128)(2,1)} %copy-done.4, bf16[227,4,1]{0,2,1:T(2,128)(2,1)S(1)} %get-tuple-element.14), dimensions={2} | concatenate | bytes 3726432 | tf_op jit(solution)/shard_map/concatenate | solution.py:33
  375.5 71.6 %all-reduce.8.cloned.1.call-done = bf16[227,2,1024]{0,2,1:T(8,128)(2,1)} async-done(((bf16[227,2,1024]{0,2,1:T(8,128)(2,1)}), bf16[227,2,1024]{0,2,1:T(8,128)(2,1)}) %all-reduce.8.cloned.1.call-update) | async-done | bytes 929808 | tf_op jit(solution)/shard_map/psum | solution.py:106
  450.1 11.2 %collective-permute-done.14 = bf16[227,1,1024]{0,2,1:T(8,128)(2,1)S(1)} collective-permute-done((bf16[227,1,1024]{0,2,1:T(8,128)(2,1)S(1)}, bf16[227,1,1024]{0,2,1:T(8,128)(2,1)S(1)}, u32[]{:S(2)}, u32[]{:S(2)}) %collective-permute-start.14) | collective-permute-done | bytes 464928 | tf_op jit(solution)/shard_map/ppermute | solution.py:29
  461.6 16.1 %gather_fusion.3 = f32[4096,227]{1,0:T(8,128)} fusion(f32[227,3072]{0,1:T(8,128)S(1)} %bitcast.217, s32[4096]{0:T(1024)S(1)} %broadcast_clamp_fusion), kind=kCustom, calls=%fused_computation.3.clone | custom fusion | bytes 7454720 | tf_op jit(solution)/shard_map/jit(_take)/gather | solution.py:74
  477.8 5.4 copy.67
  483.2 16.1 %gather_fusion.2 = f32[4096,227]{1,0:T(8,128)} fusion(f32[227,3072]{0,1:T(8,128)S(1)} %bitcast.218, s32[4096]{0:T(1024)S(1)} %broadcast_clamp_fusion.1), kind=kCustom, calls=%fused_computation.2.clone | custom fusion | bytes 7454720 | tf_op jit(solution)/shard_map/jit(_take)/gather | solution.py:73
  499.3 5.3 copy.66
  504.6 16.1 %gather_fusion.1 = f32[4096,227]{1,0:T(8,128)} fusion(f32[227,3072]{0,1:T(8,128)S(1)} %bitcast.219, s32[4096]{0:T(1024)S(1)} %broadcast_clamp_fusion.2), kind=kCustom, calls=%fused_computation.1.clone | custom fusion | bytes 7454720 | tf_op jit(solution)/shard_map/jit(_take)/gather | solution.py:72
  520.8 5.3 copy.65
  526.1 16.1 %gather_fusion = f32[4096,227]{1,0:T(8,128)} fusion(f32[227,3072]{0,1:T(8,128)S(1)} %bitcast.220, s32[4096]{0:T(1024)S(1)} %broadcast_clamp_fusion.3), kind=kCustom, calls=%fused_computation.clone | custom fusion | bytes 7454720 | tf_op jit(solution)/shard_map/jit(_take)/gather | solution.py:71
  542.2 5.3 copy.64
  547.6 9.3 %fusion.5 = bf16[227,16,256]{2,0,1:T(8,128)(2,1)} fusion(f32[16,256,227]{1,2,0:T(8,128)} %copy.67, f32[16,256,227]{1,2,0:T(8,128)} %copy.66, f32[16,256,227]{1,2,0:T(8,128)} %copy.65, f32[16,256,227]{1,2,0:T(8,128)} %copy.64, f32[16,256]{1,0:T(8,128)S(1)} %get-tuple-element.47, f32[16,256]{1,0:T(8,128)S(1)} %get-tuple-element.48, ...), kind=kLoop, calls=%fused_computation.11 | loop fusion | flops 11157504 | bytes 16818176 | tf_op jit(solution)/shard_map/convert_element_type | solution.py:81
  556.8 8.4 %all-to-all-start.1 = ((bf16[227,16,256]{2,0,1:T(8,128)(2,1)}), bf16[227,16,256]{2,0,1:T(8,128)(2,1)S(1)}, u32[]{:S(2)}, u32[]{:S(2)}) async-start(bf16[227,16,256]{2,0,1:T(8,128)(2,1)} %fusion.5), calls=%async_computation.1 | async-start | bytes 3801088 | tf_op jit(solution)/shard_map/all_to_all | solution.py:126
  567.0 20.8 %all-to-all-done.1 = bf16[227,16,256]{2,0,1:T(8,128)(2,1)S(1)} async-done(((bf16[227,16,256]{2,0,1:T(8,128)(2,1)}), bf16[227,16,256]{2,0,1:T(8,128)(2,1)S(1)}, u32[]{:S(2)}, u32[]{:S(2)}) %all-to-all-start.1) | async-done | bytes 1859616 | tf_op jit(solution)/shard_map/all_to_all | solution.py:126
  (190 shorter events, 171.5 us)
Async XLA Ops:
  7.2 35.9 %copy-start = (bf16[64,227,3,3]{1,0,3,2:T(8,128)(2,1)S(1)}, bf16[64,227,3,3]{1,0,3,2:T(8,128)(2,1)}, u32[]{:S(2)}) copy-start(bf16[64,227,3,3]{1,0,3,2:T(8,128)(2,1)} %param.12) | copy-start | bytes 784516
  7.2 147.7 %all-reduce.4.cloned.1.call-start = ((), (), s32[]{:S(2)}) async-start(), calls=%async_computation.2 | async-start | bytes 2097152 | tf_op jit(solution)/shard_map/psum | solution.py:106
  9.5 14.2 %collective-permute-start.3 = (bf16[227,1,1024]{2,0,1:T(8,128)(2,1)S(1)}, bf16[227,1,1024]{2,0,1:T(8,128)(2,1)S(1)}, u32[]{:S(2)}, u32[]{:S(2)}) collective-permute-start(bf16[227,1,1024]{2,0,1:T(8,128)(2,1)S(1)} %get-tuple-element.27), channel_id=1, source_target_pairs={{8,0},{16,8},{24,16},{32,24},{40,32},{48,40},{56,48},{64,56},{72,6... | collective-permute-start | bytes 1394696 | tf_op jit(solution)/shard_map/ppermute | solution.py:17
  10.8 13.8 %collective-permute-start.2 = (bf16[227,1,1024]{2,0,1:T(8,128)(2,1)S(1)}, bf16[227,1,1024]{2,0,1:T(8,128)(2,1)S(1)}, u32[]{:S(2)}, u32[]{:S(2)}) collective-permute-start(bf16[227,1,1024]{2,0,1:T(8,128)(2,1)S(1)} %get-tuple-element.26), channel_id=1, source_target_pairs={{0,8},{8,16},{16,24},{24,32},{32,40},{40,48},{48,56},{56,64},{64,7... | collective-permute-start | bytes 1394696 | tf_op jit(solution)/shard_map/ppermute | solution.py:16
  49.2 25.1 %copy-start.7 = (f32[2,1,1032,64]{2,3,0,1:T(8,128)}, f32[2,1,1032,64]{2,3,0,1:T(8,128)S(1)}, u32[]{:S(2)}) copy-start(f32[2,1,1032,64]{2,3,0,1:T(8,128)S(1)} %reshape.159) | copy-start | bytes 1585156
  49.4 24.8 %collective-permute-start.5 = (bf16[64,1,1024]{2,0,1:T(8,128)(2,1)S(1)}, bf16[64,1,1024]{2,0,1:T(8,128)(2,1)S(1)}, u32[]{:S(2)}, u32[]{:S(2)}) collective-permute-start(bf16[64,1,1024]{2,0,1:T(8,128)(2,1)S(1)} %get-tuple-element.41), channel_id=1, source_target_pairs={{8,0},{16,8},{24,16},{32,24},{40,32},{48,40},{56,48},{64,56},{72,6... | collective-permute-start | bytes 393224 | tf_op jit(solution)/shard_map/ppermute | solution.py:17
  50.7 23.5 %collective-permute-start.4 = (bf16[64,1,1024]{2,0,1:T(8,128)(2,1)S(1)}, bf16[64,1,1024]{2,0,1:T(8,128)(2,1)S(1)}, u32[]{:S(2)}, u32[]{:S(2)}) collective-permute-start(bf16[64,1,1024]{2,0,1:T(8,128)(2,1)S(1)} %get-tuple-element.40), channel_id=1, source_target_pairs={{0,8},{8,16},{16,24},{24,32},{32,40},{40,48},{48,56},{56,64},{64,7... | collective-permute-start | bytes 393224 | tf_op jit(solution)/shard_map/ppermute | solution.py:16
  56.5 29.9 %collective-permute-start.1 = (bf16[227,1,1024]{2,0,1:T(8,128)(2,1)}, bf16[227,1,1024]{2,0,1:T(8,128)(2,1)}, u32[]{:S(2)}, u32[]{:S(2)}) collective-permute-start(bf16[227,1,1024]{2,0,1:T(8,128)(2,1)} %get-tuple-element.29), channel_id=1, source_target_pairs={{8,0},{16,8},{24,16},{32,24},{40,32},{48,40},{56,48},{64,56},{72,6... | collective-permute-start | bytes 1394696 | tf_op jit(solution)/shard_map/ppermute | solution.py:17
  57.8 28.6 %collective-permute-start = (bf16[227,1,1024]{2,0,1:T(8,128)(2,1)}, bf16[227,1,1024]{2,0,1:T(8,128)(2,1)}, u32[]{:S(2)}, u32[]{:S(2)}) collective-permute-start(bf16[227,1,1024]{2,0,1:T(8,128)(2,1)} %get-tuple-element.28), channel_id=1, source_target_pairs={{0,8},{8,16},{16,24},{24,32},{32,40},{40,48},{48,56},{56,64},{64,7... | collective-permute-start | bytes 1394696 | tf_op jit(solution)/shard_map/ppermute | solution.py:16
  83.8 215.9 %all-reduce.6.cloned.1.call-start = ((), (), s32[]{:S(2)}) async-start(), calls=%async_computation.3 | async-start | bytes 2097152 | tf_op jit(solution)/shard_map/psum | solution.py:106
  158.0 37.3 %collective-permute-start.7 = (bf16[227,1,1024]{0,2,1:T(8,128)(2,1)}, bf16[227,1,1024]{0,2,1:T(8,128)(2,1)}, u32[]{:S(2)}, u32[]{:S(2)}) collective-permute-start(bf16[227,1,1024]{0,2,1:T(8,128)(2,1)} %get-tuple-element.25), channel_id=1, source_target_pairs={{8,0},{16,8},{24,16},{32,24},{40,32},{48,40},{56,48},{64,56},{72,6... | collective-permute-start | bytes 1394696 | tf_op jit(solution)/shard_map/ppermute | solution.py:17
  159.3 36.0 %collective-permute-start.6 = (bf16[227,1,1024]{0,2,1:T(8,128)(2,1)}, bf16[227,1,1024]{0,2,1:T(8,128)(2,1)}, u32[]{:S(2)}, u32[]{:S(2)}) collective-permute-start(bf16[227,1,1024]{0,2,1:T(8,128)(2,1)} %get-tuple-element.24), channel_id=1, source_target_pairs={{0,8},{8,16},{16,24},{24,32},{32,40},{40,48},{48,56},{56,64},{64,7... | collective-permute-start | bytes 1394696 | tf_op jit(solution)/shard_map/ppermute | solution.py:16
  217.8 5.7 collective-permute-start.9
  219.1 6.3 %collective-permute-start.8 = (bf16[64,1,1024]{2,0,1:T(8,128)(2,1)S(1)}, bf16[64,1,1024]{2,0,1:T(8,128)(2,1)S(1)}, u32[]{:S(2)}, u32[]{:S(2)}) collective-permute-start(bf16[64,1,1024]{2,0,1:T(8,128)(2,1)S(1)} %get-tuple-element.38), channel_id=1, source_target_pairs={{0,8},{8,16},{16,24},{24,32},{32,40},{40,48},{48,56},{56,64},{64,7... | collective-permute-start | bytes 393224 | tf_op jit(solution)/shard_map/ppermute | solution.py:16
  232.6 75.7 %all-to-all-start = ((s32[16,1,256]{2,1,0:T(1,128)}), s32[16,1,256]{2,1,0:T(1,128)S(1)}, u32[]{:S(2)}, u32[]{:S(2)}) async-start(s32[16,1,256]{2,1,0:T(1,128)} %all_to_all.11), calls=%async_computation | async-start | bytes 32768 | tf_op jit(solution)/shard_map/all_to_all | solution.py:100
  242.9 204.2 %all-reduce.8.cloned.1.call-start = ((), (), s32[]{:S(2)}) async-start(), calls=%async_computation.4 | async-start | bytes 2097152 | tf_op jit(solution)/shard_map/psum | solution.py:106
  302.2 12.9 %collective-permute-start.11 = (bf16[227,1,1024]{0,2,1:T(8,128)(2,1)}, bf16[227,1,1024]{0,2,1:T(8,128)(2,1)}, u32[]{:S(2)}, u32[]{:S(2)}) collective-permute-start(bf16[227,1,1024]{0,2,1:T(8,128)(2,1)} %get-tuple-element.23), channel_id=1, source_target_pairs={{8,0},{16,8},{24,16},{32,24},{40,32},{48,40},{56,48},{64,56},{72,6... | collective-permute-start | bytes 1394696 | tf_op jit(solution)/shard_map/ppermute | solution.py:17
  303.5 12.5 %collective-permute-start.10 = (bf16[227,1,1024]{0,2,1:T(8,128)(2,1)}, bf16[227,1,1024]{0,2,1:T(8,128)(2,1)}, u32[]{:S(2)}, u32[]{:S(2)}) collective-permute-start(bf16[227,1,1024]{0,2,1:T(8,128)(2,1)} %get-tuple-element.22), channel_id=1, source_target_pairs={{0,8},{8,16},{16,24},{24,32},{32,40},{40,48},{48,56},{56,64},{64,7... | collective-permute-start | bytes 1394696 | tf_op jit(solution)/shard_map/ppermute | solution.py:16
  352.7 6.8 %collective-permute-start.13 = (bf16[64,1,1024]{2,0,1:T(8,128)(2,1)S(1)}, bf16[64,1,1024]{2,0,1:T(8,128)(2,1)S(1)}, u32[]{:S(2)}, u32[]{:S(2)}) collective-permute-start(bf16[64,1,1024]{2,0,1:T(8,128)(2,1)S(1)} %get-tuple-element.37), channel_id=1, source_target_pairs={{8,0},{16,8},{24,16},{32,24},{40,32},{48,40},{56,48},{64,56},{72,6... | collective-permute-start | bytes 393224 | tf_op jit(solution)/shard_map/ppermute | solution.py:17
  354.0 6.7 %collective-permute-start.12 = (bf16[64,1,1024]{2,0,1:T(8,128)(2,1)S(1)}, bf16[64,1,1024]{2,0,1:T(8,128)(2,1)S(1)}, u32[]{:S(2)}, u32[]{:S(2)}) collective-permute-start(bf16[64,1,1024]{2,0,1:T(8,128)(2,1)S(1)} %get-tuple-element.36), channel_id=1, source_target_pairs={{0,8},{8,16},{16,24},{24,32},{32,40},{40,48},{48,56},{56,64},{64,7... | collective-permute-start | bytes 393224 | tf_op jit(solution)/shard_map/ppermute | solution.py:16
  373.0 74.2 %copy-start.9 = (bf16[227,2,1024]{0,2,1:T(8,128)(2,1)S(1)}, bf16[227,2,1024]{0,2,1:T(8,128)(2,1)}, u32[]{:S(2)}) copy-start(bf16[227,2,1024]{0,2,1:T(8,128)(2,1)} %all-reduce.6.cloned.1.call-done) | copy-start | bytes 2789380
  448.6 13.0 %copy-start.2 = (f32[227,2,1024]{0,2,1:T(8,128)}, f32[227,2,1024]{0,2,1:T(8,128)S(1)}, u32[]{:S(2)}) copy-start(f32[227,2,1024]{0,2,1:T(8,128)S(1)} %convert_add_fusion) | copy-start | bytes 5578756
  448.7 12.6 %collective-permute-start.14 = (bf16[227,1,1024]{0,2,1:T(8,128)(2,1)S(1)}, bf16[227,1,1024]{0,2,1:T(8,128)(2,1)S(1)}, u32[]{:S(2)}, u32[]{:S(2)}) collective-permute-start(bf16[227,1,1024]{0,2,1:T(8,128)(2,1)S(1)} %slice.208), channel_id=1, source_target_pairs={{8,0},{16,8},{24,16},{32,24},{40,32},{48,40},{56,48},{64,56},{72,6... | collective-permute-start | bytes 1394696 | tf_op jit(solution)/shard_map/ppermute | solution.py:29
  556.8 31.0 %all-to-all-start.1 = ((bf16[227,16,256]{2,0,1:T(8,128)(2,1)}), bf16[227,16,256]{2,0,1:T(8,128)(2,1)S(1)}, u32[]{:S(2)}, u32[]{:S(2)}) async-start(bf16[227,16,256]{2,0,1:T(8,128)(2,1)} %fusion.5), calls=%async_computation.1 | async-start | bytes 3801088 | tf_op jit(solution)/shard_map/all_to_all | solution.py:126
  (21 other events, 75.7 us)
Sparse Core Ops, SparseCore 0:
  83.9 70.8 all-reduce.3
  232.1 67.5 all-reduce.5
  375.5 71.5 all-reduce.7
where the time goes:
time: 609 us; the launch traced here: 598 us
  waiting for transfers between devices  242 us (40%)
  local copies, waits for them, and re-layouts  221 us (36%)
  starting transfers between devices  73.9 us (12%)
  other arithmetic  25.4 us (4%)
  matrix products  20.7 us (3%)
  between operations  14.8 us (2%)
    psum x3, waiting for transfers between devices, combine_sums(): lax.psum(partial_value.astype(jnp.bfloat16), 'chan').astype(jnp.float32)  193 us
    conv_general_dilated x29, local copies, waits for them, and re-layouts, convolve(): lax.conv_general_dilated(wrapped[None], kernel, (1, 1), 'VALID', dimensio...  57.7 us
    ppermute x7, starting transfers between devices, with_halo(): before = lax.ppermute(last, axis, up)  44.8 us
    concatenate x7, local copies, waits for them, and re-layouts, convolve(): jnp.concatenate([extended[:, :, -1:], extended, extended[:, :, :1]], axis=2)  35.7 us
    gather x2, local copies, waits for them, and re-layouts, interpolate(): corner_se = jnp.take(flat, (north + 1) * span + east, axis=1)  21.5 us
    gather x2, local copies, waits for them, and re-layouts, interpolate(): corner_nw = jnp.take(flat, north * span + west, axis=1)  21.5 us
    gather x2, local copies, waits for them, and re-layouts, interpolate(): corner_ne = jnp.take(flat, north * span + east, axis=1)  21.5 us
    gather x2, local copies, waits for them, and re-layouts, interpolate(): corner_sw = jnp.take(flat, (north + 1) * span + west, axis=1)  21.4 us
  transfers between devices with their start and end apart: 20, of which 11 were waited for; matrix products, arithmetic and copies ran while one was open for 9% of the time, Pallas kernels for 0%

commit v1 on v0

v1 whole, which is shorter than its diff:
```python
import jax
import jax.numpy as jnp
from jax import lax
from jax.experimental import pallas as pl
from jax.experimental.pallas import tpu as pltpu
from jax.sharding import PartitionSpec as P

MESH = pl.DeviceIdType.MESH
F32 = jnp.float32
BF16 = jnp.bfloat16

FIELDS = 227
CH = 256
NB = 16
NZ = 4
ROWS = 32
LON = 1024
OWN = 128
EDGE = 8
W = OWN + 2 * EDGE
JC = 240
CAP = 256
LATENT = 512


def dot(a, b):
    return lax.dot_general(a, b, (((1,), (0,)), ((), ())), preferred_element_type=F32)


def dot_nt(a, b):
    return lax.dot_general(a, b, (((1,), (1,)), ((), ())), preferred_element_type=F32)


def slope(u):
    s = jax.nn.sigmoid(u)
    return s * (1.0 + u * (1.0 - s))


def kernel(
    w_ref, x_ref, seed_ref, op_ref, pos_ref, sens_ref, imp_ref,
    wts, xin, sdin, xb, sdb, pre1, lat2, sh, hb, s2, s2b, sb, mid, midin, midb,
    gt, opr, posr, tent, impbuf, impin,
    wsend, wrecv, gsend, grecv, xsend, xrecv, ssend, srecv, msend, mrecv,
    psend, precv, osend, orecv, osem, isend, irecv,
):
    band = lax.axis_index("band")
    chan = lax.axis_index("chan")
    z = chan // 2
    core = chan % 2
    sib = (band, 2 * z + (1 - core))
    zp = (band, 2 * lax.rem(z + 1, NZ) + core)
    zm = (band, 2 * lax.rem(z + NZ - 1, NZ) + core)

    def at_band(d):
        return (lax.rem(band + (d + NB), NB), chan)

    barrier = pltpu.get_barrier_semaphore()
    for d in range(1, NB):
        pl.semaphore_signal(barrier, inc=1, device_id=at_band(d), device_id_type=MESH)
    for dev in (sib, zp, zm):
        pl.semaphore_signal(barrier, inc=1, device_id=dev, device_id_type=MESH)
    pl.semaphore_wait(barrier, NB - 1 + 3)

    def copy(src, dst, ss, rs, dev):
        return pltpu.make_async_remote_copy(
            src_ref=src, dst_ref=dst, send_sem=ss, recv_sem=rs, device_id=dev, device_id_type=MESH
        )

    def gather(region, half, ss, rs):
        return [
            copy(region(0), region(0), ss.at[0], rs.at[0], sib),
            copy(region(0), region(1), ss.at[1], rs.at[1], zp),
            copy(region(0), region(2), ss.at[2], rs.at[2], zm),
            copy(region(1), region(1), ss.at[3], rs.at[3], sib),
            copy(region(2), region(2), ss.at[4], rs.at[4], sib),
            copy(half(1, 0), half(3, 0), ss.at[5], rs.at[5], zp),
            copy(half(2, 1), half(3, 1), ss.at[6], rs.at[6], zm),
            copy(half(3, 0), half(3, 0), ss.at[7], rs.at[7], sib),
            copy(half(3, 1), half(3, 1), ss.at[8], rs.at[8], sib),
        ]

    lrow = pl.multiple_of(core * 64, 64)
    wcopies = gather(
        lambda q: wts.at[:, q, pl.ds(lrow, 64), :],
        lambda q, h: wts.at[pl.ds(9 * h, 9), q, pl.ds(lrow, 64), :],
        wsend, wrecv,
    )
    wts[:, 0, pl.ds(lrow, 64), :] = w_ref[...]
    for c in wcopies[:3]:
        c.start()

    xin[2 * 288:3 * 288, :] = x_ref[...].astype(BF16)
    sdin[288:2 * 288, :] = seed_ref[...].astype(BF16)
    xcopies, scopies = [], []
    for n, d in enumerate((1, -1, 2, -2)):
        xcopies.append(copy(
            xin.at[pl.ds(576, 288), :], xin.at[pl.ds((2 - d) * 288, 288), :], xsend.at[n], xrecv.at[n], at_band(d)))
    for n, d in enumerate((1, -1)):
        scopies.append(copy(
            sdin.at[pl.ds(288, 288), :], sdin.at[pl.ds((1 - d) * 288, 288), :], ssend.at[n], srecv.at[n], at_band(d)))
    for c in xcopies + scopies:
        c.start()

    def pcopy(d):
        return copy(pos_ref.at[lax.rem(band + d, NB)], posr.at[d], psend.at[d], precv.at[d], at_band(d))

    def ocopy(d):
        return copy(op_ref.at[lax.rem(band + d, NB)], opr.at[d], osend.at[d], orecv.at[d], at_band(d))

    posr[0] = pos_ref[band]
    own_op = pltpu.make_async_copy(op_ref.at[band], opr.at[0], osem)
    own_op.start()
    for d in range(1, NB):
        pcopy(d).start()
    for d in range(1, NB):
        ocopy(d).start()

    def shift3(dst, rows, width, first, flip):
        for r in range(rows):
            at = 2 * band + (first + r)
            live = jnp.logical_and(at >= 0, at < ROWS)
            for b in range(3):
                v = sh[8 + r * W + b - 1:8 + r * W + b - 1 + W, :width]
                lane = (2 - b if flip else b) * width
                dst[r * W:(r + 1) * W, lane:lane + width] = jnp.where(live, v, 0.0).astype(BF16)

    def rows_of(ref, base, n, width):
        return jnp.concatenate([ref[pl.ds(pl.multiple_of(base + a * W, 16), n), :width] for a in range(3)], axis=1)

    def taps(first, flip, q, nq, axis):
        parts = []
        for a in range(3):
            k = first + 3 * (2 - a if flip else a)
            if axis == 0:
                parts.append(wts[k:k + 3, q:q + nq].reshape(3 * nq * 128, CH))
            else:
                parts += [wts[k + b, q:q + nq].reshape(nq * 128, CH) for b in range(3)]
        return jnp.concatenate(parts, axis=axis)

    for c in xcopies + scopies:
        c.wait_recv()
    sh[8:8 + 10 * W, :CH] = xin[...].astype(F32)
    shift3(xb, 10, CH, -4, False)
    sh[8:8 + 6 * W, :CH] = sdin[...].astype(F32)
    shift3(sdb, 6, CH, -2, True)
    s2[0:288, :] = xin[288:576, :].astype(F32)
    s2[288:576, :] = x_ref[...]
    s2[576:864, :] = xin[864:1152, :].astype(F32)

    def first_half(q, nq):
        width, off = nq * 128, q * 128

        def conv1(t, _):
            base = pl.multiple_of(t * 288, 16)
            p = dot_nt(rows_of(xb, base, 288, 3 * CH), taps(0, False, q, nq, 1))
            pre1[pl.ds(base, 288), off:off + width] = p
            sh[pl.ds(pl.multiple_of(base + 8, 8), 288), :width] = p * jax.nn.sigmoid(p)
            return 0

        lax.fori_loop(0, 4, conv1, 0)
        shift3(hb, 8, width, -3, False)

        def conv2(t, _):
            base = pl.multiple_of(t * 288, 16)
            s2[pl.ds(base, 288), :] += dot(rows_of(hb, base, 288, 3 * width), taps(9, False, q, nq, 0))
            return 0

        lax.fori_loop(0, 3, conv2, 0)

        def back(t, _):
            base = pl.multiple_of(t * 288, 16)
            lat2[pl.ds(base, 288), off:off + width] = dot_nt(
                rows_of(sdb, base, 288, 3 * CH), taps(9, True, q, nq, 1))
            return 0

        lax.fori_loop(0, 2, back, 0)

    wcopies[0].wait_recv()
    first_half(0, 1)

    for d in range(1, NB):
        pcopy(d).wait_recv()

    def build(d, _):
        lon = (posr[d] & (4 * LON - 1)).astype(F32) * 0.25
        for q, dz in enumerate((0, NZ - 1, 1, 2)):
            at = lax.rem(z + dz, NZ) * 256
            west = (lax.broadcasted_iota(jnp.int32, (256, CAP), 0) + at).astype(F32)
            gap = jnp.abs(west - lon)
            gap = jnp.minimum(gap, LON - gap)
            tent[d, q * 256:(q + 1) * 256, :] = jnp.maximum(1.0 - gap, 0.0).astype(BF16)
        return 0

    lax.fori_loop(0, NB, build, 0)

    wcopies[1].wait_recv()
    wcopies[5].start()
    wcopies[3].start()
    wcopies[2].wait_recv()
    wcopies[6].start()
    wcopies[4].start()
    wcopies[3].wait_recv()
    wcopies[4].wait_recv()
    first_half(1, 2)
    wcopies[5].wait_recv()
    wcopies[7].start()
    wcopies[6].wait_recv()
    wcopies[8].start()
    wcopies[7].wait_recv()
    wcopies[8].wait_recv()
    first_half(3, 1)

    sh[8:8 + 6 * W, :CH] = s2[...]
    shift3(s2b, 6, CH, -2, False)

    def second(t, _):
        base = pl.multiple_of(t * 288, 16)
        p = dot_nt(rows_of(s2b, base, 288, 3 * CH), taps(0, False, 0, 4, 1))
        sh[pl.ds(pl.multiple_of(base + 8, 8), 288), :] = lat2[pl.ds(base, 288), :] * slope(p)
        return 0

    lax.fori_loop(0, 2, second, 0)
    shift3(sb, 4, LATENT, -1, True)
    mid[...] = seed_ref[...] + dot(rows_of(sb, 0, 288, 3 * LATENT), taps(0, True, 0, 4, 0))
    midin[288:576, :] = mid[...].astype(BF16)
    mcopies = [
        copy(midin.at[pl.ds(288, 288), :], midin.at[pl.ds(0, 288), :], msend.at[0], mrecv.at[0], at_band(1)),
        copy(midin.at[pl.ds(288, 288), :], midin.at[pl.ds(576, 288), :], msend.at[1], mrecv.at[1], at_band(-1)),
        copy(midin.at[pl.ds(288, W), :], midin.at[pl.ds(864, W), :], msend.at[2], mrecv.at[2], at_band(-2)),
    ]
    for c in mcopies:
        c.start()
    for c in mcopies:
        c.wait_recv()

    sh[8:8 + 7 * W, :CH] = midin[...].astype(F32)
    shift3(midb, 7, CH, -2, True)

    def first(t, _):
        base = pl.multiple_of(t * W, 16)
        v = dot_nt(rows_of(midb, base, W, 3 * CH), taps(9, True, 0, 4, 1))
        sh[pl.ds(pl.multiple_of(base + 8, 8), W), :] = v * slope(pre1[pl.ds(pl.multiple_of(base + 288, 16), W), :])
        return 0

    lax.fori_loop(0, 5, first, 0)
    shift3(sb, 5, LATENT, -1, True)
    for r in range(3):
        start = mid[r * W:(r + 1) * W, :] if r < 2 else midin[4 * W:5 * W, :].astype(F32)
        g = start + dot(rows_of(sb, r * W, W, 3 * LATENT), taps(0, True, 0, 4, 0))
        g = jnp.transpose(g[EDGE:EDGE + OWN, :])
        if r < 2:
            sens_ref[r] = g
        else:
            g = jnp.where(band < NB - 1, g, 0.0)
        gt[core, r * CH:(r + 1) * CH, :] = g.astype(BF16)

    gcopies = gather(
        lambda q: gt.at[2 * q + core],
        lambda q, h: gt.at[2 * q + core, pl.ds(384 * h, 384), :],
        gsend, grecv,
    )
    for c in gcopies[:3]:
        c.start()
    gcopies[1].wait_recv()
    gcopies[5].start()
    gcopies[3].start()
    gcopies[2].wait_recv()
    gcopies[6].start()
    gcopies[4].start()
    gcopies[5].wait_recv()
    gcopies[7].start()
    gcopies[6].wait_recv()
    gcopies[8].start()
    for n in (0, 3, 4, 7, 8):
        gcopies[n].wait_recv()

    own_op.wait()
    for d in range(1, NB):
        ocopy(d).wait_recv()

    def icopy(d):
        return copy(impbuf.at[d], impin.at[band], isend.at[d], irecv.at[d], at_band(-d))

    def observe(d, _):
        m = dot(jnp.concatenate([gt[n] for n in range(8)], axis=1), tent[d])
        row = (posr[d] // (4 * LON)).astype(F32) * 0.25
        col = jnp.maximum(1.0 - row, 0.0) * m[0:JC]
        col += jnp.maximum(1.0 - jnp.abs(row - 1.0), 0.0) * m[CH:CH + JC]
        col += jnp.maximum(row - 1.0, 0.0) * m[2 * CH:2 * CH + JC]
        impbuf[d] = jnp.sum(col * opr[d].astype(F32), axis=0, keepdims=True)
        return 0

    for d in range(NB):
        observe(d, 0)
        if d > 0:
            icopy(d).start()
    impin[band] = impbuf[0]
    for d in range(1, NB):
        pltpu.make_async_remote_copy(
            src_ref=impbuf.at[d], dst_ref=impin.at[lax.rem(band + d, NB)], send_sem=isend.at[d],
            recv_sem=irecv.at[d], device_id=at_band(-d), device_id_type=MESH).wait_recv()
    imp_ref[...] = impin[...]
    for c in wcopies + xcopies + scopies + mcopies + gcopies:
        c.wait_send()
    for d in range(1, NB):
        pcopy(d).wait_send()
        ocopy(d).wait_send()
        icopy(d).wait_send()


def fused(w, x, seed, op, pos):
    def vm(shape, dtype):
        return pltpu.VMEM(shape, dtype)

    dma = pltpu.SemaphoreType.DMA
    return pl.pallas_call(
        kernel,
        out_shape=(
            jax.ShapeDtypeStruct((2, CH, OWN), F32),
            jax.ShapeDtypeStruct((NB, 1, CAP), F32),
        ),
        in_specs=[pl.BlockSpec(memory_space=pltpu.VMEM)] * 3
        + [pl.BlockSpec(memory_space=pl.ANY), pl.BlockSpec(memory_space=pltpu.VMEM)],
        out_specs=(pl.BlockSpec(memory_space=pltpu.VMEM),) * 2,
        scratch_shapes=[
            vm((18, 4, 128, CH), BF16),
            vm((10 * W, CH), BF16),
            vm((6 * W, CH), BF16),
            vm((10 * W, 3 * CH), BF16),
            vm((6 * W, 3 * CH), BF16),
            vm((8 * W, LATENT), F32),
            vm((4 * W, LATENT), F32),
            vm((10 * W + 16, LATENT), F32),
            vm((8 * W, 3 * 256), BF16),
            vm((6 * W, CH), F32),
            vm((6 * W, 3 * CH), BF16),
            vm((5 * W, 3 * LATENT), BF16),
            vm((2 * W, CH), F32),
            vm((7 * W, CH), BF16),
            vm((7 * W, 3 * CH), BF16),
            vm((8, 3 * CH, OWN), BF16),
            vm((NB, JC, CAP), BF16),
            vm((NB, 1, CAP), jnp.int32),
            vm((NB, LON, CAP), BF16),
            vm((NB, 1, CAP), F32),
            vm((NB, 1, CAP), F32),
            dma((9,)), dma((9,)), dma((9,)), dma((9,)),
            dma((4,)), dma((4,)), dma((2,)), dma((2,)), dma((3,)), dma((3,)),
            dma((NB,)), dma((NB,)), dma((NB,)), dma((NB,)), dma, dma((NB,)), dma((NB,)),
        ],
        compiler_params=pltpu.CompilerParams(
            collective_id=0, has_side_effects=True, vmem_limit_bytes=60 * 1024 * 1024
        ),
    )(w, x, seed, op, pos)


def window(state, start, fill):
    around = jnp.concatenate([state[:, :, -EDGE:], state, state[:, :, :EDGE]], axis=2)
    part = lax.dynamic_slice_in_dim(around, start, W, 2)
    part = jnp.transpose(part, (1, 2, 0)).reshape(2 * W, FIELDS)
    ones = jnp.full((2 * W, 3), fill, F32)
    return jnp.concatenate([part, ones, jnp.zeros((2 * W, CH - FIELDS - 3), F32)], axis=1)


def local(
    analysed_fields,
    prediction_adjoint_seed,
    encoder_kernel_matrix,
    hidden_offset_term,
    decoder_kernel_matrix,
    measurement_wanted_positions,
    measurement_active_total,
    measurement_linear_operator,
):
    start = lax.axis_index("chan") * OWN
    enc = jnp.transpose(encoder_kernel_matrix, (2, 3, 0, 1)).reshape(9, 64, FIELDS)
    dec = jnp.transpose(decoder_kernel_matrix, (2, 3, 1, 0)).reshape(9, 64, FIELDS)
    high = lax.reduce_precision(hidden_offset_term, 8, 7)
    middle = lax.reduce_precision(hidden_offset_term - high, 8, 7)
    low = hidden_offset_term - high - middle
    bias = jnp.stack([high, middle, low], axis=1)[None].astype(BF16)
    bias = jnp.pad(bias, ((4, 13), (0, 0), (FIELDS, CH - FIELDS - 3)))
    w = jnp.pad(jnp.concatenate([enc, dec], axis=0), ((0, 0), (0, 0), (0, CH - FIELDS))) + bias
    op = jnp.pad(jnp.transpose(measurement_linear_operator[0, 0], (1, 0, 2)), ((0, 0), (0, JC - FIELDS), (0, 0)))
    pos = measurement_wanted_positions[0, 0][:, None, :]
    sens, imp = fused(
        w, window(analysed_fields, start, 1.0), window(prediction_adjoint_seed, start, 0.0), op, pos)
    sensitivity = jnp.transpose(sens[:, :FIELDS, :], (1, 0, 2))
    live = jnp.arange(CAP, dtype=jnp.int32)[None, :] < measurement_active_total[0, 0][:, None]
    impact = jnp.where(live, imp[:, 0, :], jnp.float32(0.0))
    return (sensitivity, impact[None, None])


def solution(mesh):
    in_specs = (
        P(None, "band", None),
        P(None, "band", None),
        P("chan", None, None, None),
        P("chan"),
        P(None, "chan", None, None),
        P("band", "chan", None, None),
        P("band", "chan", None),
        P("band", "chan", None, None, None),
    )
    out_specs = (P(None, "band", "chan"), P("band", "chan", None, None))
    return jax.shard_map(local, mesh=mesh, in_specs=in_specs, out_specs=out_specs, check_vma=False)
```

time: 609 us -> 149 us (0.24); the launches traced: 598 us -> 148 us
  waiting for transfers between devices: 242 us -> 0 us
  local copies, waits for them, and re-layouts: 221 us -> 26.6 us
  Pallas kernels: 0 us -> 117 us
  starting transfers between devices: 73.9 us -> 0 us
  other arithmetic: 25.4 us -> 3.7 us
  matrix products: 20.7 us -> 0 us
  between operations: 14.8 us -> 0.72 us
    psum x3 -> x0, waiting for transfers between devices: 193 us -> none  [combine_sums(): lax.psum(partial_value.astype(jnp.bfloat16), 'chan').astype(jnp.float32)]
    pallas_call x0 -> x1, Pallas kernels: none -> 117 us  [fused(): pl.pallas_call(kernel, out_shape=(jax.ShapeDtypeStruct((2, CH, OWN), F32)...]
    gather x8 -> x0, local copies, waits for them, and re-layouts: 85.9 us -> none  [the longest x2 21.5 us: interpolate(): corner_se = jnp.take(flat, (north + 1) * span + east, axis=1)]
    conv_general_dilated x29 -> x0, local copies, waits for them, and re-layouts: 57.7 us -> none  [convolve(): lax.conv_general_dilated(wrapped[None], kernel, (1, 1), 'VALID', dimensio...]
    ppermute x15 -> x0, starting transfers between devices: 55.1 us -> none  [the longest x7 44.8 us: with_halo(): before = lax.ppermute(last, axis, up)]
    ppermute x15 -> x0, waiting for transfers between devices: 28.7 us -> none  [the longest x7 12.7 us: with_halo(): after = lax.ppermute(first, axis, down)]
    all_to_all x2 -> x0, waiting for transfers between devices: 20.8 us -> none  [the longest x1 20.8 us: local(): lax.all_to_all(columns, 'band', split_axis=1, concat_axis=1, tiled=True)]
    conv_general_dilated x7 -> x0, matrix products: 20.7 us -> none  [convolve(): lax.conv_general_dilated(wrapped[None], kernel, (1, 1), 'VALID', dimensio...]
  transfers between devices with their start and end apart: 20 -> 0, of which waited for: 11 -> 0; matrix products, arithmetic and copies ran while one was open for 9% -> 0% of each run, Pallas kernels for 0% -> 0%
where the time goes in v1:
time: 149 us; the launch traced here: 148 us
  Pallas kernels  117 us (79%)
  local copies, waits for them, and re-layouts  26.6 us (18%)
  other arithmetic  3.7 us (2%)
    pallas_call x1, Pallas kernels, fused(): pl.pallas_call(kernel, out_shape=(jax.ShapeDtypeStruct((2, CH, OWN), F32)...  117 us
    concatenate x2, local copies, waits for them, and re-layouts, window(): jnp.concatenate([state[:, :, -EDGE:], state, state[:, :, :EDGE]], axis=2)  15.9 us

profile of v1, /device:TPU:1, one launch (start us, length us, event | category | flops | bytes accessed | tf_op | source)
XLA Modules:
  0.0 148.0 jit_solution(1220373140507429540)
XLA Ops:
  0.6 1.4 fusion.9
  2.0 7.7 %concatenate.24 = f32[227,2,1040]{2,1,0:T(2,128)S(1)} concatenate(f32[227,2,8]{2,1,0:T(2,128)S(1)} %get-tuple-element.13, f32[227,2,1024]{2,1,0:T(2,128)} %param.8, f32[227,2,8]{2,1,0:T(2,128)S(1)} %get-tuple-element.12), dimensions={2} | concatenate | bytes 3777280 | tf_op jit(solution)/shard_map/concatenate | solution.py:358
  9.7 1.4 fusion.8
  11.1 8.2 %concatenate.26 = f32[227,2,1040]{2,1,0:T(2,128)} concatenate(f32[227,2,8]{2,1,0:T(2,128)S(1)} %get-tuple-element.11, f32[227,2,1024]{2,1,0:T(2,128)} %param.9, f32[227,2,8]{2,1,0:T(2,128)S(1)} %get-tuple-element.10), dimensions={2} | concatenate | bytes 3777280 | tf_op jit(solution)/shard_map/concatenate | solution.py:358
  19.3 2.1 %dynamic-slice_bitcast_fusion = (f32[2,144,227]{1,0,2:T(2,128)S(1)}, f32[2,144,227]{1,0,2:T(2,128)S(1)}) fusion(f32[227,2,1040]{2,1,0:T(2,128)} %concatenate.26, s32[]{:T(128)S(6)} %select_n.15, f32[227,2,1040]{2,1,0:T(2,128)S(1)} %concatenate.24), kind=kLoop, calls=%fused_computation.6 | loop fusion | bytes 1046020 | tf_op jit(solution)/shard_map/transpose | solution.py:360
  21.5 0.0 copy-start
  21.5 0.2 copy.20
  21.7 0.2 copy.19
  21.9 0.1 pad.16.clone
  22.0 0.1 pad.19.clone
  22.0 0.1 pad.20.clone
  22.1 0.9 maximum_maximum_fusion.1
  23.0 0.1 copy.18
  23.1 2.0 %fusion.3.w_ref = bf16[18,64,256]{2,1,0:T(8,128)(2,1)} fusion(bf16[9,64,227]{2,1,0:T(8,128)(2,1)} %bitcast.33, bf16[9,64,227]{2,1,0:T(8,128)(2,1)} %bitcast.34, bf16[1,64,3]{2,1,0:T(8,128)(2,1)S(1)} %copy.18), kind=kLoop, calls=%fused_computation.5 | loop fusion | flops 2654208 | bytes 1113216 | tf_op jit(solution)/shard_map/add | solution.py:383
  25.1 0.6 copy.25
  25.8 0.0 copy-start.1
  25.8 1.4 pad.14.op_ref
  27.2 0.0 copy-done.1
  27.2 0.6 broadcast_in_dim_squeeze.4.pos_ref
  27.8 116.9 %shard_map.98 = (f32[2,256,128]{2,1,0:T(8,128)}, f32[16,1,256]{2,1,0:T(1,128)}) custom-call(bf16[18,64,256]{2,1,0:T(8,128)(2,1)} %fusion.3.w_ref, f32[288,256]{1,0:T(8,128)} %get-tuple-element.15.x_ref, f32[288,256]{1,0:T(8,128)} %get-tuple-element.14.seed_ref, bf16[16,240,256]{2,1,0:T(8,128)(2,1)} %pad.14.op_ref, s32[16,1,256]{2,1,0:T(1,128)} %broadcast_in_dim_squeeze.4.pos_ref), custom_call_target="tpu_custom_call" | custom-call | tf_op jit(solution)/shard_map/pallas_call | solution.py:316
  144.8 1.0 slice_bitcast_fusion
  145.7 0.8 copy.22
  146.5 0.8 compare_select_fusion
  147.4 0.6 copy.23
  (10 shorter events, 0.0 us)
Async XLA Ops:
  19.3 3.7 %copy-start.3 = (f32[64]{0:T(128)S(1)}, f32[64]{0:T(128)}, u32[]{:S(2)}) copy-start(f32[64]{0:T(128)} %param.11) | copy-start | bytes 772
  21.5 3.7 %copy-start = (bf16[1,1,227,16,256]{4,3,2,1,0:T(8,128)(2,1)S(1)}, bf16[1,1,227,16,256]{4,3,2,1,0:T(8,128)(2,1)}, u32[]{:S(2)}) copy-start(bf16[1,1,227,16,256]{4,3,2,1,0:T(8,128)(2,1)} %param.15) | copy-start | bytes 5578756
  25.8 1.4 copy-start.1
  27.8 118.7 %copy-start.2 = (s32[1,1,16]{2,1,0:T(1,128)S(1)}, s32[1,1,16]{2,1,0:T(1,128)}, u32[]{:S(2)}) copy-start(s32[1,1,16]{2,1,0:T(1,128)} %param.14) | copy-start | bytes 196

commit v2 on v1

v2 whole, which is shorter than its diff:
```python
import jax
import jax.numpy as jnp
from jax import lax
from jax.experimental import pallas as pl
from jax.experimental.pallas import tpu as pltpu
from jax.sharding import PartitionSpec as P

MESH = pl.DeviceIdType.MESH
F32 = jnp.float32
BF16 = jnp.bfloat16

FIELDS = 227
CH = 256
NB = 16
NZ = 4
ROWS = 32
LON = 1024
OWN = 128
EDGE = 8
W = OWN + 2 * EDGE
JC = 240
CAP = 256
LATENT = 512
OP_FIRST = 8


def dot(a, b):
    return lax.dot_general(a, b, (((1,), (0,)), ((), ())), preferred_element_type=F32)


def dot_nt(a, b):
    return lax.dot_general(a, b, (((1,), (1,)), ((), ())), preferred_element_type=F32)


def slope(u):
    s = jax.nn.sigmoid(u)
    return s * (1.0 + u * (1.0 - s))


def kernel(
    enc_ref, dec_ref, bias_ref, x_ref, seed_ref, op_ref, pos_ref, sens_ref, imp_ref,
    wts, raw, x, seed, xin, sdin, stin, midin, xb, sdb, pre1, lat2, sh, hb, s2, sb, mid,
    gt, opr, posb, posr, tent, part, impbuf, impin,
    rsem, wsend, wrecv, gsend, grecv, hsend, hrecv, xsend, xrecv,
    psend, precv, osend, orecv, osem, isend, irecv,
):
    band = lax.axis_index("band")
    chan = lax.axis_index("chan")
    z = chan // 2
    core = chan % 2
    sib = (band, 2 * z + (1 - core))
    zp = (band, 2 * lax.rem(z + 1, NZ) + core)
    zm = (band, 2 * lax.rem(z + NZ - 1, NZ) + core)

    def at_band(d):
        return (lax.rem(band + (d + NB), NB), chan)

    fetches = []
    for n, ref in enumerate((x_ref, seed_ref)):
        for t in range(3):
            block = pl.ds(pl.multiple_of(lax.rem(chan + (t + 7), 8) * OWN, OWN), OWN)
            fetches.append(pltpu.make_async_copy(
                ref.at[:, :, block], raw.at[n, pl.ds(0, FIELDS), :, pl.ds(t * OWN, OWN)], rsem.at[n, t]))
    for c in fetches:
        c.start()

    barrier = pltpu.get_barrier_semaphore()
    for d in range(1, NB):
        pl.semaphore_signal(barrier, inc=1, device_id=at_band(d), device_id_type=MESH)
    for dev in (sib, zp, zm):
        pl.semaphore_signal(barrier, inc=1, device_id=dev, device_id_type=MESH)

    lrow = pl.multiple_of(core * 64, 64)
    for n, ref in enumerate((enc_ref, dec_ref)):
        for k in range(9):
            wts[9 * n + k, 0, pl.ds(lrow, 64), 0:128] = ref[k, :, 0:128]
            rest = jnp.concatenate([ref[k, :, 128:FIELDS], jnp.zeros((64, CH - FIELDS), BF16)], axis=1)
            if n == 0 and k == 4:
                eye = lax.broadcasted_iota(jnp.int32, (64, 64), 0) == lax.broadcasted_iota(jnp.int32, (64, 64), 1)
                bias = jnp.sum(jnp.where(eye, bias_ref[...], 0.0), axis=1, keepdims=True)
                high = bias.astype(BF16).astype(F32)
                middle = (bias - high).astype(BF16).astype(F32)
                low = bias - high - middle
                lane = lax.broadcasted_iota(jnp.int32, (64, 128), 1) + 128
                terms = jnp.where(lane == FIELDS, high, jnp.where(lane == FIELDS + 1, middle, low))
                terms = jnp.where(jnp.logical_and(lane >= FIELDS, lane < FIELDS + 3), terms, 0.0)
                rest = (rest.astype(F32) + terms).astype(BF16)
            wts[9 * n + k, 0, pl.ds(lrow, 64), 128:256] = rest

    pl.semaphore_wait(barrier, NB - 1 + 3)

    def copy(src, dst, ss, rs, dev):
        return pltpu.make_async_remote_copy(
            src_ref=src, dst_ref=dst, send_sem=ss, recv_sem=rs, device_id=dev, device_id_type=MESH
        )

    def gather(region, half, ss, rs):
        return [
            copy(region(0), region(0), ss.at[0], rs.at[0], sib),
            copy(region(0), region(1), ss.at[1], rs.at[1], zp),
            copy(region(0), region(2), ss.at[2], rs.at[2], zm),
            copy(region(1), region(1), ss.at[3], rs.at[3], sib),
            copy(region(2), region(2), ss.at[4], rs.at[4], sib),
            copy(half(1, 0), half(3, 0), ss.at[5], rs.at[5], zp),
            copy(half(2, 1), half(3, 1), ss.at[6], rs.at[6], zm),
            copy(half(3, 0), half(3, 0), ss.at[7], rs.at[7], sib),
            copy(half(3, 1), half(3, 1), ss.at[8], rs.at[8], sib),
        ]

    wcopies = gather(
        lambda q: wts.at[:, q, pl.ds(lrow, 64), :],
        lambda q, h: wts.at[pl.ds(9 * h, 9), q, pl.ds(lrow, 64), :],
        wsend, wrecv,
    )
    for c in wcopies[:3]:
        c.start()

    def exchange(ref, n):
        own = ref.at[pl.ds(288, 288), :]
        return [
            copy(own, ref.at[pl.ds(0, 288), :], xsend.at[n, 0], xrecv.at[n, 0], at_band(1)),
            copy(own, ref.at[pl.ds(576, 288), :], xsend.at[n, 1], xrecv.at[n, 1], at_band(-1)),
        ]

    halos = [exchange(ref, n) for n, ref in enumerate((xin, sdin, stin, midin))]
    for n, (ref, own, fill) in enumerate(((x, xin, 1.0), (seed, sdin, 0.0))):
        for t in range(3):
            fetches[3 * n + t].wait()
        channel = lax.broadcasted_iota(jnp.int32, (CH - 224, 3 * OWN), 0) + 224
        for r in range(2):
            tail = raw[n, 224:CH, r, :]
            tail = jnp.where(channel < FIELDS, tail, jnp.where(channel < FIELDS + 3, fill, 0.0))
            rows = jnp.concatenate([raw[n, 0:224, r, :], tail], axis=0)
            ref[r * W:r * W + EDGE, :] = jnp.transpose(rows[:, 0:OWN])[OWN - EDGE:, :]
            ref[r * W + EDGE:r * W + EDGE + OWN, :] = jnp.transpose(rows[:, OWN:2 * OWN])
            ref[r * W + EDGE + OWN:(r + 1) * W, :] = jnp.transpose(rows[:, 2 * OWN:3 * OWN])[:EDGE, :]
        own[288:576, :] = ref[...].astype(BF16)
        for c in halos[n]:
            c.start()

    def pcopy(d):
        return copy(posb.at[lax.rem(band + d, NB)], posr.at[d], psend.at[d], precv.at[d], at_band(d))

    def ocopy(d):
        return copy(op_ref.at[lax.rem(band + d, NB)], opr.at[d], osend.at[d], orecv.at[d], at_band(d))

    for k in range(NB):
        posb[k] = pos_ref[k:k + 1, :]
    posr[0] = posb[band]
    for d in range(1, NB):
        pcopy(d).start()
    own_op = pltpu.make_async_copy(op_ref.at[band], opr.at[0], osem)
    own_op.start()

    def shift3(dst, rows, width, first, flip):
        for r in range(rows):
            at = 2 * band + (first + r)
            live = jnp.logical_and(at >= 0, at < ROWS)
            for b in range(3):
                v = sh[8 + r * W + b - 1:8 + r * W + b - 1 + W, :width]
                lane = (2 - b if flip else b) * width
                dst[r * W:(r + 1) * W, lane:lane + width] = jnp.where(live, v, 0.0).astype(BF16)

    def spread(dst, ref, flip):
        sh[8:8 + 6 * W, :CH] = ref[...].astype(F32)
        shift3(dst, 6, CH, -2, flip)

    def rows_of(ref, n, width):
        return jnp.concatenate([ref[a * W:a * W + n, :width] for a in range(3)], axis=1)

    def taps(first, flip, lat, axis):
        parts = []
        for a in range(3):
            k = first + 3 * (2 - a if flip else a)
            if axis == 0:
                part_ = wts[k:k + 3, lat]
                parts.append(part_.reshape(part_.shape[0] * part_.shape[1] * part_.shape[2], CH))
            else:
                for b in range(3):
                    part_ = wts[k + b, lat]
                    parts.append(part_.reshape(part_.shape[0] * part_.shape[1], CH))
        return jnp.concatenate(parts, axis=axis)

    for c in halos[0]:
        c.wait_recv()
    spread(xb, xin, False)
    s2[...] = x[...]

    def first_half(q, nq, parts):
        width, off = nq * 128, q * 128
        lat = pl.ds(q, nq)
        if "state" in parts:
            p = dot_nt(rows_of(xb, 4 * W, 3 * CH), taps(0, False, lat, 1))
            pre1[:, off:off + width] = p
            sh[8:8 + 4 * W, :width] = p * jax.nn.sigmoid(p)
            shift3(hb, 4, width, -1, False)
            s2[...] += dot(rows_of(hb, 2 * W, 3 * width), taps(9, False, lat, 0))
        if "seed" in parts:
            lat2[:, off:off + width] = dot_nt(rows_of(sdb, 4 * W, 3 * CH), taps(9, True, lat, 1))

    wcopies[0].wait_recv()
    first_half(0, 1, ("state",))
    for c in halos[1]:
        c.wait_recv()
    spread(sdb, sdin, True)
    for d in range(1, OP_FIRST):
        ocopy(d).start()
    first_half(0, 1, ("seed",))

    for d in range(1, NB):
        pcopy(d).wait_recv()

    def build(d, _):
        lon = (posr[d] & (4 * LON - 1)).astype(F32) * 0.25
        for q, dz in enumerate((0, NZ - 1, 1, 2)):
            at = lax.rem(z + dz, NZ) * 256
            west = (lax.broadcasted_iota(jnp.int32, (256, CAP), 0) + at).astype(F32)
            gap = jnp.abs(west - lon)
            gap = jnp.minimum(gap, LON - gap)
            tent[d, q * 256:(q + 1) * 256, :] = jnp.maximum(1.0 - gap, 0.0).astype(BF16)
        return 0

    lax.fori_loop(0, NB, build, 0)

    wcopies[1].wait_recv()
    wcopies[5].start()
    wcopies[3].start()
    wcopies[2].wait_recv()
    wcopies[6].start()
    wcopies[4].start()
    wcopies[3].wait_recv()
    wcopies[4].wait_recv()
    first_half(1, 2, ("state", "seed"))
    wcopies[5].wait_recv()
    wcopies[7].start()
    wcopies[6].wait_recv()
    wcopies[8].start()
    wcopies[7].wait_recv()
    wcopies[8].wait_recv()
    first_half(3, 1, ("state",))
    stin[288:576, :] = s2[...].astype(BF16)
    for c in halos[2]:
        c.start()
    first_half(3, 1, ("seed",))

    for c in halos[2]:
        c.wait_recv()
    spread(xb, stin, False)

    def second(t, _):
        off = pl.multiple_of(t * 256, 256)
        p = dot_nt(rows_of(xb, 4 * W, 3 * CH), taps(0, False, pl.ds(2 * t, 2), 1))
        sh[8:8 + 4 * W, pl.ds(off, 256)] = lat2[:, pl.ds(off, 256)] * slope(p)
        return 0

    lax.fori_loop(0, 2, second, 0)
    shift3(sb, 4, LATENT, -1, True)
    mid[...] = seed[...] + dot(rows_of(sb, 2 * W, 3 * LATENT), taps(0, True, pl.ds(0, 4), 0))
    midin[288:576, :] = mid[...].astype(BF16)
    for c in halos[3]:
        c.start()
    for c in halos[3]:
        c.wait_recv()
    for d in range(OP_FIRST, NB):
        ocopy(d).start()

    spread(sdb, midin, True)

    def first(t, _):
        off = pl.multiple_of(t * 256, 256)
        v = dot_nt(rows_of(sdb, 4 * W, 3 * CH), taps(9, True, pl.ds(2 * t, 2), 1))
        sh[8:8 + 4 * W, pl.ds(off, 256)] = v * slope(pre1[:, pl.ds(off, 256)])
        return 0

    lax.fori_loop(0, 2, first, 0)
    shift3(sb, 4, LATENT, -1, True)
    mid[...] += dot(rows_of(sb, 2 * W, 3 * LATENT), taps(0, True, pl.ds(0, 4), 0))
    for r in range(2):
        g = jnp.transpose(mid[r * W + EDGE:r * W + EDGE + OWN, :])
        sens_ref[:, r, :] = g[:FIELDS]
        gt[core, r * JC:(r + 1) * JC, :] = g[:JC].astype(BF16)

    below = copy(gt.at[core, pl.ds(0, JC), :], gt.at[core, pl.ds(2 * JC, JC), :], hsend, hrecv, at_band(-1))
    below.start()
    own_rows = gather(
        lambda q: gt.at[2 * q + core, pl.ds(0, 2 * JC), :],
        lambda q, h: gt.at[2 * q + core, pl.ds(JC * h, JC), :],
        gsend.at[0], grecv.at[0],
    )
    next_row = gather(
        lambda q: gt.at[2 * q + core, pl.ds(2 * JC, JC), :],
        lambda q, h: gt.at[2 * q + core, pl.ds(2 * JC + 112 * h, 112 + 16 * h), :],
        gsend.at[1], grecv.at[1],
    )
    for c in own_rows[:3]:
        c.start()
    below.wait_recv()
    gt[core, 2 * JC:3 * JC, :] = jnp.where(band < NB - 1, gt[core, 2 * JC:3 * JC, :].astype(F32), 0.0).astype(BF16)
    for c in next_row[:3]:
        c.start()

    own_rows[0].wait_recv()

    def near(d, _):
        part[d] = dot(jnp.concatenate([gt[n, 0:2 * JC] for n in range(2)], axis=1), tent[d, 0:256])
        return 0

    lax.fori_loop(0, NB, near, 0)

    for g in (own_rows, next_row):
        g[1].wait_recv()
        g[5].start()
        g[3].start()
        g[2].wait_recv()
        g[6].start()
        g[4].start()
    own_rows[3].wait_recv()
    own_rows[4].wait_recv()
    for g in (own_rows, next_row):
        g[5].wait_recv()
        g[7].start()
        g[6].wait_recv()
        g[8].start()

    def beside(d, _):
        part[d] += dot(jnp.concatenate([gt[n, 0:2 * JC] for n in range(2, 6)], axis=1), tent[d, 256:768])
        return 0

    lax.fori_loop(0, NB, beside, 0)

    own_rows[7].wait_recv()
    own_rows[8].wait_recv()
    for n in (0, 3, 4, 7, 8):
        next_row[n].wait_recv()

    def icopy(d):
        return copy(impbuf.at[d], impin.at[band], isend.at[d], irecv.at[d], at_band(-d))

    def observe(d):
        m = part[d] + dot(jnp.concatenate([gt[n, 0:2 * JC] for n in range(6, 8)], axis=1), tent[d, 768:1024])
        m2 = dot(jnp.concatenate([gt[n, 2 * JC:3 * JC] for n in range(8)], axis=1), tent[d])
        row = (posr[d] // (4 * LON)).astype(F32) * 0.25
        col = jnp.maximum(1.0 - row, 0.0) * m[0:JC]
        col += jnp.maximum(1.0 - jnp.abs(row - 1.0), 0.0) * m[JC:2 * JC]
        col += jnp.maximum(row - 1.0, 0.0) * m2
        impbuf[d] = jnp.sum(col * opr[d].astype(F32), axis=0, keepdims=True)

    def answer(d, _):
        ocopy(d).wait_recv()
        observe(d)
        icopy(d).start()
        return 0

    lax.fori_loop(1, NB, answer, 0)
    own_op.wait()
    observe(0)
    impin[band] = impbuf[0]
    for d in range(1, NB):
        copy(impbuf.at[d], impin.at[lax.rem(band + d, NB)], isend.at[d], irecv.at[d], at_band(-d)).wait_recv()
    for k in range(NB):
        imp_ref[k:k + 1, :] = impin[k]
    for c in wcopies + sum(halos, []) + own_rows + next_row + [below]:
        c.wait_send()
    for d in range(1, NB):
        pcopy(d).wait_send()
        ocopy(d).wait_send()
        icopy(d).wait_send()


def fused(enc, dec, bias, x, seed, op, pos):
    def vm(shape, dtype):
        return pltpu.VMEM(shape, dtype)

    vmem, anywhere = pl.BlockSpec(memory_space=pltpu.VMEM), pl.BlockSpec(memory_space=pl.ANY)
    dma = pltpu.SemaphoreType.DMA
    return pl.pallas_call(
        kernel,
        out_shape=(
            jax.ShapeDtypeStruct((FIELDS, 2, OWN), F32),
            jax.ShapeDtypeStruct((NB, CAP), F32),
        ),
        in_specs=[vmem, vmem, vmem, anywhere, anywhere, anywhere, vmem],
        out_specs=(vmem, vmem),
        scratch_shapes=[
            vm((18, 4, 128, CH), BF16),
            vm((2, CH, 2, 3 * OWN), F32),
            vm((2 * W, CH), F32),
            vm((2 * W, CH), F32),
            vm((6 * W, CH), BF16),
            vm((6 * W, CH), BF16),
            vm((6 * W, CH), BF16),
            vm((6 * W, CH), BF16),
            vm((6 * W, 3 * CH), BF16),
            vm((6 * W, 3 * CH), BF16),
            vm((4 * W, LATENT), F32),
            vm((4 * W, LATENT), F32),
            vm((6 * W + 16, LATENT), F32),
            vm((4 * W, 3 * 256), BF16),
            vm((2 * W, CH), F32),
            vm((4 * W, 3 * LATENT), BF16),
            vm((2 * W, CH), F32),
            vm((8, 3 * JC, OWN), BF16),
            vm((NB, JC, CAP), BF16),
            vm((NB, 1, CAP), jnp.int32),
            vm((NB, 1, CAP), jnp.int32),
            vm((NB, LON, CAP), BF16),
            vm((NB, 2 * JC, CAP), F32),
            vm((NB, 1, CAP), F32),
            vm((NB, 1, CAP), F32),
            dma((2, 3)), dma((9,)), dma((9,)), dma((2, 9)), dma((2, 9)), dma, dma, dma((4, 2)), dma((4, 2)),
            dma((NB,)), dma((NB,)), dma((NB,)), dma((NB,)), dma, dma((NB,)), dma((NB,)),
        ],
        compiler_params=pltpu.CompilerParams(
            collective_id=0, has_side_effects=True, vmem_limit_bytes=60 * 1024 * 1024
        ),
    )(enc, dec, bias, x, seed, op, pos)


def local(
    analysed_fields,
    prediction_adjoint_seed,
    encoder_kernel_matrix,
    hidden_offset_term,
    decoder_kernel_matrix,
    measurement_wanted_positions,
    measurement_active_total,
    measurement_linear_operator,
):
    enc = jnp.transpose(encoder_kernel_matrix, (2, 3, 0, 1)).reshape(9, 64, FIELDS)
    dec = jnp.transpose(decoder_kernel_matrix, (2, 3, 1, 0)).reshape(9, 64, FIELDS)
    op = jnp.pad(jnp.transpose(measurement_linear_operator[0, 0], (1, 0, 2)), ((0, 0), (0, JC - FIELDS), (0, 0)))
    sensitivity, imp = fused(
        enc, dec, hidden_offset_term[None], analysed_fields, prediction_adjoint_seed, op,
        measurement_wanted_positions[0, 0])
    live = jnp.arange(CAP, dtype=jnp.int32)[None, :] < measurement_active_total[0, 0][:, None]
    impact = jnp.where(live, imp, jnp.float32(0.0))
    return (sensitivity, impact[None, None])


def solution(mesh):
    in_specs = (
        P(None, "band", None),
        P(None, "band", None),
        P("chan", None, None, None),
        P("chan"),
        P(None, "chan", None, None),
        P("band", "chan", None, None),
        P("band", "chan", None),
        P("band", "chan", None, None, None),
    )
    out_specs = (P(None, "band", "chan"), P("band", "chan", None, None))
    return jax.shard_map(local, mesh=mesh, in_specs=in_specs, out_specs=out_specs, check_vma=False)
```

time: 149 us -> 112 us (0.75)
  local copies, waits for them, and re-layouts: 26.6 us -> 5.2 us
  Pallas kernels: 117 us -> 103 us
  other arithmetic: 3.7 us -> 1.39 us
    concatenate x5 -> x0, local copies, waits for them, and re-layouts: 16.1 us -> none  [the longest x2 15.9 us: window(): jnp.concatenate([state[:, :, -EDGE:], state, state[:, :, :EDGE]], axis=2)]
    pallas_call x1, Pallas kernels: 117 us -> 103 us  [fused(): pl.pallas_call(kernel, out_shape=(jax.ShapeDtypeStruct((FIELDS, 2, OWN),...]
    transpose x4 -> x0, local copies, waits for them, and re-layouts: 3.48 us -> none  [the longest x3 2.52 us: window(): part = jnp.transpose(part, (1, 2, 0)).reshape(2 * W, FIELDS)]
    slice x2 -> x0, local copies, waits for them, and re-layouts: 2.75 us -> none  [window(): state[:, :, :EDGE]]
    add x1 -> x0, other arithmetic: 2 us -> none  [local(): jnp.pad(jnp.concatenate([enc, dec], axis=0), ((0, 0), (0, 0), (0, CH - FI...]
    unnamed x11 -> x4, local copies, waits for them, and re-layouts: 2.06 us -> 3.78 us
where the time goes in v2:
time: 112 us; the launch traced here: 111 us
  Pallas kernels  103 us (92%)
  local copies, waits for them, and re-layouts  5.2 us (5%)
  other arithmetic  1.39 us (1%)
    pallas_call x1, Pallas kernels, fused(): pl.pallas_call(kernel, out_shape=(jax.ShapeDtypeStruct((FIELDS, 2, OWN),...  103 us
    unnamed x4, local copies, waits for them, and re-layouts  3.78 us

profile of v2, /device:TPU:1, one launch (start us, length us, event | category | flops | bytes accessed | tf_op | source)
XLA Modules:
  0.0 110.6 jit_solution(14759241137832390196)
XLA Ops:
  0.6 2.1 %copy.12 = bf16[1,1,227,16,256]{4,2,3,1,0:T(8,128)(2,1)S(1)} copy(bf16[1,1,227,16,256]{4,3,2,1,0:T(8,128)(2,1)} %param.15) | data formatting | bytes 3719168 | tf_op args[7]
  2.8 1.4 %pad.4.op_ref = bf16[16,240,256]{2,1,0:T(8,128)(2,1)} pad(bf16[16,227,256]{2,1,0:T(8,128)(2,1)S(1)} %bitcast.16, bf16[]{:T(256)} %constant.1.clone.1), padding=0_0x0_13x0_0 | pad | bytes 3825666 | tf_op jit(solution)/shard_map/jit(_pad)/pad | solution.py:431
  4.2 0.0 copy-start
  4.2 103.4 %shard_map.95 = (f32[227,2,128]{2,1,0:T(2,128)}, f32[16,256]{1,0:T(8,128)}) custom-call(bf16[9,64,227]{2,1,0:T(8,128)(2,1)} %bitcast.17, bf16[9,64,227]{2,1,0:T(8,128)(2,1)} %bitcast.18, f32[1,64]{1,0:T(1,128)} %bitcast.20, f32[227,2,1024]{2,1,0:T(2,128)} %x_ref.1, f32[227,2,1024]{2,1,0:T(2,128)} %seed_ref.1, bf16[16,240,256]{2,1,0:T(8,128)(2,1)} %pad.4.op_ref, ...), custom_call_target="tpu_custom_call" | custom-call | tf_op jit(solution)/shard_map/pallas_call | solution.py:376
  107.6 0.0 copy-done
  107.6 1.4 %select_bitcast_fusion = f32[1,1,16,256]{3,2,1,0:T(8,128)} fusion(f32[16,256]{1,0:T(8,128)} %get-tuple-element.5, s32[16]{0:T(128)S(1)} %bitcast.21), kind=kLoop, calls=%fused_computation.1 | loop fusion | flops 8192 | bytes 32832 | tf_op jit(solution)/shard_map/broadcast_in_dim | solution.py:437
  109.0 1.6 %copy.14 = f32[227,2,128]{2,1,0:T(2,128)} copy(f32[227,2,128]{2,1,0:T(2,128)} %get-tuple-element.8) | data formatting | bytes 464896
Async XLA Ops:
  4.2 103.4 %copy-start = (s32[1,1,16]{2,1,0:T(1,128)S(1)}, s32[1,1,16]{2,1,0:T(1,128)}, u32[]{:S(2)}) copy-start(s32[1,1,16]{2,1,0:T(1,128)} %param.14) | copy-start | bytes 196

commit v3 on v2

--- a/solution.py
+++ b/solution.py
@@ -21,7 +21,9 @@
 JC = 240
 CAP = 256
 LATENT = 512
-OP_FIRST = 8
+BESIDE_FIRST = 4
+AWAY = (0, 4, 12, 8, 1, 15, 2, 14, 3, 13, 5, 11, 6, 10, 7, 9)
+EARLY = 8
 
 
 def dot(a, b):
@@ -40,8 +42,8 @@
 def kernel(
     enc_ref, dec_ref, bias_ref, x_ref, seed_ref, op_ref, pos_ref, sens_ref, imp_ref,
     wts, raw, x, seed, xin, sdin, stin, midin, xb, sdb, pre1, lat2, sh, hb, s2, sb, mid,
-    gt, opr, posb, posr, tent, part, impbuf, impin,
-    rsem, wsend, wrecv, gsend, grecv, hsend, hrecv, xsend, xrecv,
+    gt, low, opr, posb, posr, tent, part, impbuf, impin,
+    rsem, wsend, wrecv, gsend, grecv, xsend, xrecv,
     psend, precv, osend, orecv, osem, isend, irecv,
 ):
     band = lax.axis_index("band")
@@ -65,9 +67,9 @@
         c.start()
 
     barrier = pltpu.get_barrier_semaphore()
-    for d in range(1, NB):
-        pl.semaphore_signal(barrier, inc=1, device_id=at_band(d), device_id_type=MESH)
-    for dev in (sib, zp, zm):
+    across = [(lax.rem(band + NB + d, NB), 2 * lax.rem(z + dz, NZ) + core) for d in (-1, 0, 1) for dz in (1, 2, 3)]
+    partners = [at_band(d) for d in range(1, NB)] + [sib] + across
+    for dev in partners:
         pl.semaphore_signal(barrier, inc=1, device_id=dev, device_id_type=MESH)
 
     lrow = pl.multiple_of(core * 64, 64)
@@ -80,14 +82,14 @@
                 bias = jnp.sum(jnp.where(eye, bias_ref[...], 0.0), axis=1, keepdims=True)
                 high = bias.astype(BF16).astype(F32)
                 middle = (bias - high).astype(BF16).astype(F32)
-                low = bias - high - middle
+                least = bias - high - middle
                 lane = lax.broadcasted_iota(jnp.int32, (64, 128), 1) + 128
-                terms = jnp.where(lane == FIELDS, high, jnp.where(lane == FIELDS + 1, middle, low))
+                terms = jnp.where(lane == FIELDS, high, jnp.where(lane == FIELDS + 1, middle, least))
                 terms = jnp.where(jnp.logical_and(lane >= FIELDS, lane < FIELDS + 3), terms, 0.0)
                 rest = (rest.astype(F32) + terms).astype(BF16)
             wts[9 * n + k, 0, pl.ds(lrow, 64), 128:256] = rest
 
-    pl.semaphore_wait(barrier, NB - 1 + 3)
+    pl.semaphore_wait(barrier, len(partners))
 
     def copy(src, dst, ss, rs, dev):
         return pltpu.make_async_remote_copy(
@@ -138,19 +140,21 @@
         for c in halos[n]:
             c.start()
 
-    def pcopy(d):
-        return copy(posb.at[lax.rem(band + d, NB)], posr.at[d], psend.at[d], precv.at[d], at_band(d))
-
-    def ocopy(d):
-        return copy(op_ref.at[lax.rem(band + d, NB)], opr.at[d], osend.at[d], orecv.at[d], at_band(d))
+    def pcopy(k):
+        return copy(posb.at[lax.rem(band + AWAY[k], NB)], posr.at[k], psend.at[k], precv.at[k], at_band(AWAY[k]))
+
+    def ocopy(k):
+        return copy(op_ref.at[lax.rem(band + AWAY[k], NB)], opr.at[k], osend.at[k], orecv.at[k], at_band(AWAY[k]))
 
     for k in range(NB):
         posb[k] = pos_ref[k:k + 1, :]
     posr[0] = posb[band]
-    for d in range(1, NB):
-        pcopy(d).start()
+    for k in range(1, NB):
+        pcopy(k).start()
     own_op = pltpu.make_async_copy(op_ref.at[band], opr.at[0], osem)
     own_op.start()
+    for k in range(1, EARLY):
+        ocopy(k).start()
 
     def shift3(dst, rows, width, first, flip):
         for r in range(rows):
@@ -181,6 +185,27 @@
                     parts.append(part_.reshape(part_.shape[0] * part_.shape[1], CH))
         return jnp.concatenate(parts, axis=axis)
 
+    for d in range(1, NB):
+        pcopy(d).wait_recv()
+
+    def build(d, _):
+        lon = (posr[d] & (4 * LON - 1)).astype(F32) * 0.25
+        for q, dz in enumerate((0, NZ - 1, 1, 2)):
+            at = lax.rem(z + dz, NZ) * 256
+            west = (lax.broadcasted_iota(jnp.int32, (256, CAP), 0) + at).astype(F32)
+            gap = jnp.abs(west - lon)
+            gap = jnp.minimum(gap, LON - gap)
+            tent[d, q * 256:(q + 1) * 256, :] = jnp.maximum(1.0 - gap, 0.0).astype(BF16)
+        return 0
+
+    lax.fori_loop(0, NB, build, 0)
+
+    wcopies[1].wait_recv()
+    wcopies[5].start()
+    wcopies[3].start()
+    wcopies[2].wait_recv()
+    wcopies[6].start()
+    wcopies[4].start()
     for c in halos[0]:
         c.wait_recv()
     spread(xb, xin, False)
@@ -198,39 +223,14 @@
         if "seed" in parts:
             lat2[:, off:off + width] = dot_nt(rows_of(sdb, 4 * W, 3 * CH), taps(9, True, lat, 1))
 
-    wcopies[0].wait_recv()
-    first_half(0, 1, ("state",))
     for c in halos[1]:
         c.wait_recv()
     spread(sdb, sdin, True)
-    for d in range(1, OP_FIRST):
-        ocopy(d).start()
-    first_half(0, 1, ("seed",))
-
-    for d in range(1, NB):
-        pcopy(d).wait_recv()
-
-    def build(d, _):
-        lon = (posr[d] & (4 * LON - 1)).astype(F32) * 0.25
-        for q, dz in enumerate((0, NZ - 1, 1, 2)):
-            at = lax.rem(z + dz, NZ) * 256
-            west = (lax.broadcasted_iota(jnp.int32, (256, CAP), 0) + at).astype(F32)
-            gap = jnp.abs(west - lon)
-            gap = jnp.minimum(gap, LON - gap)
-            tent[d, q * 256:(q + 1) * 256, :] = jnp.maximum(1.0 - gap, 0.0).astype(BF16)
-        return 0
-
-    lax.fori_loop(0, NB, build, 0)
-
-    wcopies[1].wait_recv()
-    wcopies[5].start()
-    wcopies[3].start()
-    wcopies[2].wait_recv()
-    wcopies[6].start()
-    wcopies[4].start()
+    wcopies[0].wait_recv()
+
     wcopies[3].wait_recv()
     wcopies[4].wait_recv()
-    first_half(1, 2, ("state", "seed"))
+    first_half(0, 3, ("state", "seed"))
     wcopies[5].wait_recv()
     wcopies[7].start()
     wcopies[6].wait_recv()
@@ -261,8 +261,8 @@
         c.start()
     for c in halos[3]:
         c.wait_recv()
-    for d in range(OP_FIRST, NB):
-        ocopy(d).start()
+    for k in range(EARLY, NB):
+        ocopy(k).start()
 
     spread(sdb, midin, True)
 
@@ -280,91 +280,81 @@
         sens_ref[:, r, :] = g[:FIELDS]
         gt[core, r * JC:(r + 1) * JC, :] = g[:JC].astype(BF16)
 
-    below = copy(gt.at[core, pl.ds(0, JC), :], gt.at[core, pl.ds(2 * JC, JC), :], hsend, hrecv, at_band(-1))
-    below.start()
-    own_rows = gather(
-        lambda q: gt.at[2 * q + core, pl.ds(0, 2 * JC), :],
-        lambda q, h: gt.at[2 * q + core, pl.ds(JC * h, JC), :],
-        gsend.at[0], grecv.at[0],
-    )
-    next_row = gather(
-        lambda q: gt.at[2 * q + core, pl.ds(2 * JC, JC), :],
-        lambda q, h: gt.at[2 * q + core, pl.ds(2 * JC + 112 * h, 112 + 16 * h), :],
-        gsend.at[1], grecv.at[1],
-    )
-    for c in own_rows[:3]:
+    low[...] = jnp.where(band > 0, gt[core, 0:JC, :].astype(F32), 0.0).astype(BF16)
+    own_rows, next_row = [], []
+    for q, dz in enumerate((0, 1, NZ - 1, 2)):
+        there = 2 * lax.rem(z + dz, NZ) + core
+        if q > 0:
+            own_rows.append(copy(
+                gt.at[core, pl.ds(0, 2 * JC), :], gt.at[2 * q + core, pl.ds(0, 2 * JC), :],
+                gsend.at[0, q], grecv.at[0, q], (band, there)))
+        next_row.append(copy(
+            low, gt.at[2 * q + core, pl.ds(2 * JC, JC), :], gsend.at[1, q], grecv.at[1, q],
+            (lax.rem(band + NB - 1, NB), there)))
+    own_shared = [copy(
+        gt.at[2 * q + core, pl.ds(0, 2 * JC), :], gt.at[2 * q + core, pl.ds(0, 2 * JC), :],
+        gsend.at[0, 4 + q], grecv.at[0, 4 + q], sib) for q in range(4)]
+    next_shared = [copy(
+        gt.at[2 * q + core, pl.ds(2 * JC, JC), :], gt.at[2 * q + core, pl.ds(2 * JC, JC), :],
+        gsend.at[1, 4 + q], grecv.at[1, 4 + q], sib) for q in range(4)]
+    for c in own_rows + next_row + own_shared[:1]:
         c.start()
-    below.wait_recv()
-    gt[core, 2 * JC:3 * JC, :] = jnp.where(band < NB - 1, gt[core, 2 * JC:3 * JC, :].astype(F32), 0.0).astype(BF16)
-    for c in next_row[:3]:
-        c.start()
-
-    own_rows[0].wait_recv()
+    own_shared[0].wait_recv()
 
     def near(d, _):
         part[d] = dot(jnp.concatenate([gt[n, 0:2 * JC] for n in range(2)], axis=1), tent[d, 0:256])
         return 0
 
     lax.fori_loop(0, NB, near, 0)
-
-    for g in (own_rows, next_row):
-        g[1].wait_recv()
-        g[5].start()
-        g[3].start()
-        g[2].wait_recv()
-        g[6].start()
-        g[4].start()
-    own_rows[3].wait_recv()
-    own_rows[4].wait_recv()
-    for g in (own_rows, next_row):
-        g[5].wait_recv()
-        g[7].start()
-        g[6].wait_recv()
-        g[8].start()
+    for q in range(1, 4):
+        own_rows[q - 1].wait_recv()
+        own_shared[q].start()
+    for q in range(1, 4):
+        own_shared[q].wait_recv()
 
     def beside(d, _):
-        part[d] += dot(jnp.concatenate([gt[n, 0:2 * JC] for n in range(2, 6)], axis=1), tent[d, 256:768])
-        return 0
-
-    lax.fori_loop(0, NB, beside, 0)
-
-    own_rows[7].wait_recv()
-    own_rows[8].wait_recv()
-    for n in (0, 3, 4, 7, 8):
-        next_row[n].wait_recv()
-
-    def icopy(d):
-        return copy(impbuf.at[d], impin.at[band], isend.at[d], irecv.at[d], at_band(-d))
-
-    def observe(d):
-        m = part[d] + dot(jnp.concatenate([gt[n, 0:2 * JC] for n in range(6, 8)], axis=1), tent[d, 768:1024])
+        part[d] += dot(jnp.concatenate([gt[n, 0:2 * JC] for n in range(2, 8)], axis=1), tent[d, 256:1024])
+        return 0
+
+    lax.fori_loop(0, BESIDE_FIRST, beside, 0)
+    for q in range(4):
+        next_row[q].wait_recv()
+        next_shared[q].start()
+    lax.fori_loop(BESIDE_FIRST, NB, beside, 0)
+    for q in range(4):
+        next_shared[q].wait_recv()
+
+    def icopy(k):
+        return copy(impbuf.at[k], impin.at[band], isend.at[k], irecv.at[k], at_band(-AWAY[k]))
+
+    def observe(d, _):
+        m = part[d]
         m2 = dot(jnp.concatenate([gt[n, 2 * JC:3 * JC] for n in range(8)], axis=1), tent[d])
         row = (posr[d] // (4 * LON)).astype(F32) * 0.25
         col = jnp.maximum(1.0 - row, 0.0) * m[0:JC]
         col += jnp.maximum(1.0 - jnp.abs(row - 1.0), 0.0) * m[JC:2 * JC]
         col += jnp.maximum(row - 1.0, 0.0) * m2
         impbuf[d] = jnp.sum(col * opr[d].astype(F32), axis=0, keepdims=True)
-
-    def answer(d, _):
-        ocopy(d).wait_recv()
-        observe(d)
-        icopy(d).start()
-        return 0
-
-    lax.fori_loop(1, NB, answer, 0)
+        return 0
+
     own_op.wait()
-    observe(0)
+    for lo, hi in ((0, EARLY), (EARLY, 12), (12, NB)):
+        for k in range(max(lo, 1), hi):
+            ocopy(k).wait_recv()
+        lax.fori_loop(lo, hi, observe, 0)
+        for k in range(max(lo, 1), hi):
+            icopy(k).start()
     impin[band] = impbuf[0]
-    for d in range(1, NB):
-        copy(impbuf.at[d], impin.at[lax.rem(band + d, NB)], isend.at[d], irecv.at[d], at_band(-d)).wait_recv()
+    for k in range(1, NB):
+        copy(impbuf.at[k], impin.at[lax.rem(band + AWAY[k], NB)], isend.at[k], irecv.at[k], at_band(-AWAY[k])).wait_recv()
     for k in range(NB):
         imp_ref[k:k + 1, :] = impin[k]
-    for c in wcopies + sum(halos, []) + own_rows + next_row + [below]:
+    for c in wcopies + sum(halos, []) + own_rows + own_shared + next_row + next_shared:
         c.wait_send()
-    for d in range(1, NB):
-        pcopy(d).wait_send()
-        ocopy(d).wait_send()
-        icopy(d).wait_send()
+    for k in range(1, NB):
+        pcopy(k).wait_send()
+        ocopy(k).wait_send()
+        icopy(k).wait_send()
 
 
 def fused(enc, dec, bias, x, seed, op, pos):
@@ -395,11 +385,12 @@
             vm((4 * W, LATENT), F32),
             vm((4 * W, LATENT), F32),
             vm((6 * W + 16, LATENT), F32),
-            vm((4 * W, 3 * 256), BF16),
+            vm((4 * W, 3 * 384), BF16),
             vm((2 * W, CH), F32),
             vm((4 * W, 3 * LATENT), BF16),
             vm((2 * W, CH), F32),
             vm((8, 3 * JC, OWN), BF16),
+            vm((JC, OWN), BF16),
             vm((NB, JC, CAP), BF16),
             vm((NB, 1, CAP), jnp.int32),
             vm((NB, 1, CAP), jnp.int32),
@@ -407,7 +398,7 @@
             vm((NB, 2 * JC, CAP), F32),
             vm((NB, 1, CAP), F32),
             vm((NB, 1, CAP), F32),
-            dma((2, 3)), dma((9,)), dma((9,)), dma((2, 9)), dma((2, 9)), dma, dma, dma((4, 2)), dma((4, 2)),
+            dma((2, 3)), dma((9,)), dma((9,)), dma((2, 8)), dma((2, 8)), dma((4, 2)), dma((4, 2)),
             dma((NB,)), dma((NB,)), dma((NB,)), dma((NB,)), dma, dma((NB,)), dma((NB,)),
         ],
         compiler_params=pltpu.CompilerParams(

time: 112 us -> 96.3 us (0.86); the launches traced: 111 us -> 96.1 us
  Pallas kernels: 103 us -> 88.8 us
    pallas_call x1, Pallas kernels: 103 us -> 88.8 us  [fused(): pl.pallas_call(kernel, out_shape=(jax.ShapeDtypeStruct((FIELDS, 2, OWN),...]
where the time goes in v3:
time: 96.3 us; the launch traced here: 96.1 us
  Pallas kernels  88.8 us (92%)
  local copies, waits for them, and re-layouts  5.2 us (5%)
  other arithmetic  1.39 us (1%)
    pallas_call x1, Pallas kernels, fused(): pl.pallas_call(kernel, out_shape=(jax.ShapeDtypeStruct((FIELDS, 2, OWN),...  88.8 us
    unnamed x4, local copies, waits for them, and re-layouts  3.78 us

profile of v3, /device:TPU:1, one launch (start us, length us, event | category | flops | bytes accessed | tf_op | source)
XLA Modules:
  0.0 96.1 jit_solution(4565364706361558416)
XLA Ops:
  0.6 2.1 %copy.12 = bf16[1,1,227,16,256]{4,2,3,1,0:T(8,128)(2,1)S(1)} copy(bf16[1,1,227,16,256]{4,3,2,1,0:T(8,128)(2,1)} %param.15) | data formatting | bytes 3719168 | tf_op args[7]
  2.8 1.4 %pad.4.op_ref = bf16[16,240,256]{2,1,0:T(8,128)(2,1)} pad(bf16[16,227,256]{2,1,0:T(8,128)(2,1)S(1)} %bitcast.16, bf16[]{:T(256)} %constant.1.clone.1), padding=0_0x0_13x0_0 | pad | bytes 3825666 | tf_op jit(solution)/shard_map/jit(_pad)/pad | solution.py:422
  4.2 0.0 copy-start
  4.2 88.8 %shard_map.95 = (f32[227,2,128]{2,1,0:T(2,128)}, f32[16,256]{1,0:T(8,128)}) custom-call(bf16[9,64,227]{2,1,0:T(8,128)(2,1)} %bitcast.17, bf16[9,64,227]{2,1,0:T(8,128)(2,1)} %bitcast.18, f32[1,64]{1,0:T(1,128)} %bitcast.20, f32[227,2,1024]{2,1,0:T(2,128)} %x_ref.1, f32[227,2,1024]{2,1,0:T(2,128)} %seed_ref.1, bf16[16,240,256]{2,1,0:T(8,128)(2,1)} %pad.4.op_ref, ...), custom_call_target="tpu_custom_call" | custom-call | tf_op jit(solution)/shard_map/pallas_call | solution.py:366
  93.0 0.0 copy-done
  93.0 1.4 %select_bitcast_fusion = f32[1,1,16,256]{3,2,1,0:T(8,128)} fusion(f32[16,256]{1,0:T(8,128)} %get-tuple-element.5, s32[16]{0:T(128)S(1)} %bitcast.21), kind=kLoop, calls=%fused_computation.1 | loop fusion | flops 8192 | bytes 32832 | tf_op jit(solution)/shard_map/broadcast_in_dim | solution.py:428
  94.4 1.6 %copy.14 = f32[227,2,128]{2,1,0:T(2,128)} copy(f32[227,2,128]{2,1,0:T(2,128)} %get-tuple-element.8) | data formatting | bytes 464896
Async XLA Ops:
  4.2 88.8 %copy-start = (s32[1,1,16]{2,1,0:T(1,128)S(1)}, s32[1,1,16]{2,1,0:T(1,128)}, u32[]{:S(2)}) copy-start(s32[1,1,16]{2,1,0:T(1,128)} %param.14) | copy-start | bytes 196

commit v4 on v3

--- a/solution.py
+++ b/solution.py
@@ -21,9 +21,8 @@
 JC = 240
 CAP = 256
 LATENT = 512
-BESIDE_FIRST = 4
 AWAY = (0, 4, 12, 8, 1, 15, 2, 14, 3, 13, 5, 11, 6, 10, 7, 9)
-EARLY = 8
+EARLY = 12
 
 
 def dot(a, b):
@@ -42,7 +41,7 @@
 def kernel(
     enc_ref, dec_ref, bias_ref, x_ref, seed_ref, op_ref, pos_ref, sens_ref, imp_ref,
     wts, raw, x, seed, xin, sdin, stin, midin, xb, sdb, pre1, lat2, sh, hb, s2, sb, mid,
-    gt, low, opr, posb, posr, tent, part, impbuf, impin,
+    gt, low, opw, opt, opr, posb, posr, tent, impbuf, impin,
     rsem, wsend, wrecv, gsend, grecv, xsend, xrecv,
     psend, precv, osend, orecv, osem, isend, irecv,
 ):
@@ -63,7 +62,8 @@
             block = pl.ds(pl.multiple_of(lax.rem(chan + (t + 7), 8) * OWN, OWN), OWN)
             fetches.append(pltpu.make_async_copy(
                 ref.at[:, :, block], raw.at[n, pl.ds(0, FIELDS), :, pl.ds(t * OWN, OWN)], rsem.at[n, t]))
-    for c in fetches:
+    op_fetch = pltpu.make_async_copy(op_ref, opw.at[pl.ds(0, FIELDS)], osem)
+    for c in fetches + [op_fetch]:
         c.start()
 
     barrier = pltpu.get_barrier_semaphore()
@@ -144,17 +144,22 @@
         return copy(posb.at[lax.rem(band + AWAY[k], NB)], posr.at[k], psend.at[k], precv.at[k], at_band(AWAY[k]))
 
     def ocopy(k):
-        return copy(op_ref.at[lax.rem(band + AWAY[k], NB)], opr.at[k], osend.at[k], orecv.at[k], at_band(AWAY[k]))
+        return copy(opt.at[lax.rem(band + AWAY[k], NB)], opr.at[k], osend.at[k], orecv.at[k], at_band(AWAY[k]))
 
     for k in range(NB):
         posb[k] = pos_ref[k:k + 1, :]
     posr[0] = posb[band]
     for k in range(1, NB):
         pcopy(k).start()
-    own_op = pltpu.make_async_copy(op_ref.at[band], opr.at[0], osem)
-    own_op.start()
-    for k in range(1, EARLY):
-        ocopy(k).start()
+    op_fetch.wait()
+    opw[FIELDS:JC] = jnp.zeros((JC - FIELDS, NB, CAP), BF16)
+
+    def by_band(t, _):
+        at = pl.ds(pl.multiple_of(16 * t, 16), 16)
+        opt[:, at, :] = jnp.transpose(opw[at].astype(F32), (1, 0, 2)).astype(BF16)
+        return 0
+
+    lax.fori_loop(0, JC // 16, by_band, 0)
 
     def shift3(dst, rows, width, first, flip):
         for r in range(rows):
@@ -200,6 +205,8 @@
 
     lax.fori_loop(0, NB, build, 0)
 
+    for k in range(1, EARLY):
+        ocopy(k).start()
     wcopies[1].wait_recv()
     wcopies[5].start()
     wcopies[3].start()
@@ -299,45 +306,34 @@
         gsend.at[1, 4 + q], grecv.at[1, 4 + q], sib) for q in range(4)]
     for c in own_rows + next_row + own_shared[:1]:
         c.start()
+    next_row[0].wait_recv()
+    next_shared[0].start()
     own_shared[0].wait_recv()
-
-    def near(d, _):
-        part[d] = dot(jnp.concatenate([gt[n, 0:2 * JC] for n in range(2)], axis=1), tent[d, 0:256])
-        return 0
-
-    lax.fori_loop(0, NB, near, 0)
+    next_shared[0].wait_recv()
+
     for q in range(1, 4):
         own_rows[q - 1].wait_recv()
         own_shared[q].start()
     for q in range(1, 4):
-        own_shared[q].wait_recv()
-
-    def beside(d, _):
-        part[d] += dot(jnp.concatenate([gt[n, 0:2 * JC] for n in range(2, 8)], axis=1), tent[d, 256:1024])
-        return 0
-
-    lax.fori_loop(0, BESIDE_FIRST, beside, 0)
-    for q in range(4):
         next_row[q].wait_recv()
         next_shared[q].start()
-    lax.fori_loop(BESIDE_FIRST, NB, beside, 0)
-    for q in range(4):
+    for q in range(1, 4):
+        own_shared[q].wait_recv()
         next_shared[q].wait_recv()
 
     def icopy(k):
         return copy(impbuf.at[k], impin.at[band], isend.at[k], irecv.at[k], at_band(-AWAY[k]))
 
     def observe(d, _):
-        m = part[d]
-        m2 = dot(jnp.concatenate([gt[n, 2 * JC:3 * JC] for n in range(8)], axis=1), tent[d])
+        m = dot(jnp.concatenate([gt[n] for n in range(8)], axis=1), tent[d])
         row = (posr[d] // (4 * LON)).astype(F32) * 0.25
         col = jnp.maximum(1.0 - row, 0.0) * m[0:JC]
         col += jnp.maximum(1.0 - jnp.abs(row - 1.0), 0.0) * m[JC:2 * JC]
-        col += jnp.maximum(row - 1.0, 0.0) * m2
+        col += jnp.maximum(row - 1.0, 0.0) * m[2 * JC:3 * JC]
         impbuf[d] = jnp.sum(col * opr[d].astype(F32), axis=0, keepdims=True)
         return 0
 
-    own_op.wait()
+    opr[0] = opt[band]
     for lo, hi in ((0, EARLY), (EARLY, 12), (12, NB)):
         for k in range(max(lo, 1), hi):
             ocopy(k).wait_recv()
@@ -391,11 +387,12 @@
             vm((2 * W, CH), F32),
             vm((8, 3 * JC, OWN), BF16),
             vm((JC, OWN), BF16),
+            vm((JC, NB, CAP), BF16),
+            vm((NB, JC, CAP), BF16),
             vm((NB, JC, CAP), BF16),
             vm((NB, 1, CAP), jnp.int32),
             vm((NB, 1, CAP), jnp.int32),
             vm((NB, LON, CAP), BF16),
-            vm((NB, 2 * JC, CAP), F32),
             vm((NB, 1, CAP), F32),
             vm((NB, 1, CAP), F32),
             dma((2, 3)), dma((9,)), dma((9,)), dma((2, 8)), dma((2, 8)), dma((4, 2)), dma((4, 2)),
@@ -419,7 +416,7 @@
 ):
     enc = jnp.transpose(encoder_kernel_matrix, (2, 3, 0, 1)).reshape(9, 64, FIELDS)
     dec = jnp.transpose(decoder_kernel_matrix, (2, 3, 1, 0)).reshape(9, 64, FIELDS)
-    op = jnp.pad(jnp.transpose(measurement_linear_operator[0, 0], (1, 0, 2)), ((0, 0), (0, JC - FIELDS), (0, 0)))
+    op = measurement_linear_operator[0, 0]
     sensitivity, imp = fused(
         enc, dec, hidden_offset_term[None], analysed_fields, prediction_adjoint_seed, op,
         measurement_wanted_positions[0, 0])

time: 96.3 us -> 89.6 us (0.930)
  local copies, waits for them, and re-layouts: 5.2 us -> 1.65 us
  Pallas kernels: 88.8 us -> 85.5 us
    pallas_call x1, Pallas kernels: 88.8 us -> 85.5 us  [fused(): pl.pallas_call(kernel, out_shape=(jax.ShapeDtypeStruct((FIELDS, 2, OWN),...]
    unnamed x4 -> x3, local copies, waits for them, and re-layouts: 3.78 us -> 1.65 us
    pad x1 -> x0, local copies, waits for them, and re-layouts: 1.42 us -> none  [local(): jnp.pad(jnp.transpose(measurement_linear_operator[0, 0], (1, 0, 2)), ((0,...]
where the time goes in v4:
time: 89.6 us; the launch traced here: 89.2 us
  Pallas kernels  85.5 us (95%)
  local copies, waits for them, and re-layouts  1.65 us (2%)
  other arithmetic  1.39 us (2%)
    pallas_call x1, Pallas kernels, fused(): pl.pallas_call(kernel, out_shape=(jax.ShapeDtypeStruct((FIELDS, 2, OWN),...  85.5 us

profile of v4, /device:TPU:1, one launch (start us, length us, event | category | flops | bytes accessed | tf_op | source)
XLA Modules:
  0.0 89.2 jit_solution(13385069613412412221)
XLA Ops:
  0.6 0.0 copy-start
  0.6 85.5 %shard_map.95 = (f32[227,2,128]{2,1,0:T(2,128)}, f32[16,256]{1,0:T(8,128)}) custom-call(bf16[9,64,227]{2,1,0:T(8,128)(2,1)} %bitcast.13, bf16[9,64,227]{2,1,0:T(8,128)(2,1)} %bitcast.14, f32[1,64]{1,0:T(1,128)} %bitcast.16, f32[227,2,1024]{2,1,0:T(2,128)} %x_ref.1, f32[227,2,1024]{2,1,0:T(2,128)} %seed_ref.1, bf16[227,16,256]{2,1,0:T(8,128)(2,1)} %bitcast.12, ...), custom_call_target="tpu_custom_call" | custom-call | tf_op jit(solution)/shard_map/pallas_call | solution.py:362
  86.1 0.0 copy-done
  86.1 1.4 %select_bitcast_fusion = f32[1,1,16,256]{3,2,1,0:T(8,128)} fusion(f32[16,256]{1,0:T(8,128)} %get-tuple-element.5, s32[16]{0:T(128)S(1)} %bitcast.17), kind=kLoop, calls=%fused_computation | loop fusion | flops 8192 | bytes 32832 | tf_op jit(solution)/shard_map/broadcast_in_dim | solution.py:425
  87.5 1.6 %copy.11 = f32[227,2,128]{2,1,0:T(2,128)} copy(f32[227,2,128]{2,1,0:T(2,128)} %get-tuple-element.8) | data formatting | bytes 464896
Async XLA Ops:
  0.6 85.5 %copy-start = (s32[1,1,16]{2,1,0:T(1,128)S(1)}, s32[1,1,16]{2,1,0:T(1,128)}, u32[]{:S(2)}) copy-start(s32[1,1,16]{2,1,0:T(1,128)} %param.14) | copy-start | bytes 196

commit v5 on v4

--- a/solution.py
+++ b/solution.py
@@ -39,7 +39,7 @@
 
 
 def kernel(
-    enc_ref, dec_ref, bias_ref, x_ref, seed_ref, op_ref, pos_ref, sens_ref, imp_ref,
+    enc_ref, dec_ref, bias_ref, x_ref, seed_ref, op_ref, pos_ref, live_ref, sens_ref, imp_ref,
     wts, raw, x, seed, xin, sdin, stin, midin, xb, sdb, pre1, lat2, sh, hb, s2, sb, mid,
     gt, low, opw, opt, opr, posb, posr, tent, impbuf, impin,
     rsem, wsend, wrecv, gsend, grecv, xsend, xrecv,
@@ -343,8 +343,11 @@
     impin[band] = impbuf[0]
     for k in range(1, NB):
         copy(impbuf.at[k], impin.at[lax.rem(band + AWAY[k], NB)], isend.at[k], irecv.at[k], at_band(-AWAY[k])).wait_recv()
-    for k in range(NB):
-        imp_ref[k:k + 1, :] = impin[k]
+    diagonal = lax.broadcasted_iota(jnp.int32, (NB, NB), 0) == lax.broadcasted_iota(jnp.int32, (NB, NB), 1)
+    total = jnp.sum(jnp.where(diagonal, live_ref[...].astype(F32), 0.0), axis=1, keepdims=True)
+    answers = jnp.concatenate([impin[k] for k in range(NB)], axis=0)
+    slots = lax.broadcasted_iota(jnp.int32, (NB, CAP), 1).astype(F32)
+    imp_ref[...] = jnp.where(slots < total, answers, 0.0)
     for c in wcopies + sum(halos, []) + own_rows + own_shared + next_row + next_shared:
         c.wait_send()
     for k in range(1, NB):
@@ -353,7 +356,7 @@
         icopy(k).wait_send()
 
 
-def fused(enc, dec, bias, x, seed, op, pos):
+def fused(enc, dec, bias, x, seed, op, pos, live):
     def vm(shape, dtype):
         return pltpu.VMEM(shape, dtype)
 
@@ -365,7 +368,7 @@
             jax.ShapeDtypeStruct((FIELDS, 2, OWN), F32),
             jax.ShapeDtypeStruct((NB, CAP), F32),
         ),
-        in_specs=[vmem, vmem, vmem, anywhere, anywhere, anywhere, vmem],
+        in_specs=[vmem, vmem, vmem, anywhere, anywhere, anywhere, vmem, vmem],
         out_specs=(vmem, vmem),
         scratch_shapes=[
             vm((18, 4, 128, CH), BF16),
@@ -401,7 +404,7 @@
         compiler_params=pltpu.CompilerParams(
             collective_id=0, has_side_effects=True, vmem_limit_bytes=60 * 1024 * 1024
         ),
-    )(enc, dec, bias, x, seed, op, pos)
+    )(enc, dec, bias, x, seed, op, pos, live)
 
 
 def local(
@@ -419,10 +422,8 @@
     op = measurement_linear_operator[0, 0]
     sensitivity, imp = fused(
         enc, dec, hidden_offset_term[None], analysed_fields, prediction_adjoint_seed, op,
-        measurement_wanted_positions[0, 0])
-    live = jnp.arange(CAP, dtype=jnp.int32)[None, :] < measurement_active_total[0, 0][:, None]
-    impact = jnp.where(live, imp, jnp.float32(0.0))
-    return (sensitivity, impact[None, None])
+        measurement_wanted_positions[0, 0], measurement_active_total[0])
+    return (sensitivity, imp[None, None])
 
 
 def solution(mesh):

time: 89.6 us -> 89.6 us (level)
  other arithmetic: 1.39 us -> 0 us
  local copies, waits for them, and re-layouts: 1.65 us -> 2.97 us
    broadcast_in_dim x1 -> x0, other arithmetic: 1.39 us -> none  [local(): return (sensitivity, impact[None, None])]
    unnamed x3 -> x2, local copies, waits for them, and re-layouts: 1.65 us -> 2.97 us
where the time goes in v5:
time: 89.6 us; the launch traced here: 89.2 us
  Pallas kernels  85.6 us (96%)
  local copies, waits for them, and re-layouts  2.97 us (3%)
    pallas_call x1, Pallas kernels, fused(): pl.pallas_call(kernel, out_shape=(jax.ShapeDtypeStruct((FIELDS, 2, OWN),...  85.6 us
    unnamed x2, local copies, waits for them, and re-layouts  2.97 us

profile of v5, /device:TPU:1, one launch (start us, length us, event | category | flops | bytes accessed | tf_op | source)
XLA Modules:
  0.0 89.2 jit_solution(14995062235620981224)
XLA Ops:
  0.6 85.6 %shard_map.95 = (f32[227,2,128]{2,1,0:T(2,128)}, f32[16,256]{1,0:T(8,128)}) custom-call(bf16[9,64,227]{2,1,0:T(8,128)(2,1)} %bitcast.12, bf16[9,64,227]{2,1,0:T(8,128)(2,1)} %bitcast.13, f32[1,64]{1,0:T(1,128)} %bitcast.16, f32[227,2,1024]{2,1,0:T(2,128)} %x_ref.1, f32[227,2,1024]{2,1,0:T(2,128)} %seed_ref.1, bf16[227,16,256]{2,1,0:T(8,128)(2,1)} %bitcast.11, ...), custom_call_target="tpu_custom_call" | custom-call | tf_op jit(solution)/shard_map/pallas_call | solution.py:365
  86.2 1.6 %copy.12 = f32[227,2,128]{2,1,0:T(2,128)} copy(f32[227,2,128]{2,1,0:T(2,128)} %get-tuple-element.8) | data formatting | bytes 464896
  87.9 1.3 %copy.13 = f32[1,1,16,256]{3,2,1,0:T(8,128)} copy(f32[1,1,16,256]{3,2,1,0:T(8,128)} %bitcast.15) | data formatting | bytes 32768
